TPU v7x, 256 devices: a whole 4x4x8 slice. The times are simulated.
256 devices in a mesh: dp: 32 (over z, x_hi, core), weight: 8 (over y, x_lo).
Axes of the slice: x: 4 (x_hi: 2, x_lo: 2; x = x_hi * 2 + x_lo), y: 4, z: 8, core: 2. Of those that a mesh axis runs over, the one named last changes fastest.
Arguments:
- tokens: bfloat16 [1024, 4096], P('weight'), may hold values from -6 to 6
- cotangent: bfloat16 [1024, 4096], P('weight'), may hold values from -6 to 6
- step_lengths: int32 [8, 4], P('weight'), may hold values from 1 to 64, 128 in all within a row
- step_labels: int32 [8, 4], P('weight'), may hold values from 0 to 1
- gate_weight: bfloat16 [16384, 4096], P(('dp', 'weight')), may hold values from -0.09375 to 0.09375
- up_weight: bfloat16 [16384, 4096], P(('dp', 'weight')), may hold values from -0.09375 to 0.09375
- down_weight: bfloat16 [16384, 4096], P(('dp', 'weight')), may hold values from -0.046875 to 0.046875
Outputs:
- input_grad: bfloat16 [1024, 4096], P('weight', 'dp')
- gate_grad: float32 [16384, 4096], P(('dp', 'weight'))
- up_grad: float32 [16384, 4096], P(('dp', 'weight'))
- down_grad: float32 [16384, 4096], P(('dp', 'weight'))
All inputs are finite; a program needn't handle non-finite values.
Results may differ from a plain program's by a relative error of at most 0.0057.
Values may be sent and summed in bfloat16 or wider, within the bound.
A program may use at most 128 MiB of HBM per device.

v0:
```python
import jax
import jax.numpy as jnp
from jax import lax
from jax.sharding import PartitionSpec as P


def shifted(value, axis, steps):
    count = lax.axis_size(axis)
    pairs = [(source, (source + steps) % count) for source in range(count)]
    return lax.ppermute(value, axis, pairs)


def contract_rows(left, right):
    return lax.dot_general(
        left, right, (((0,), (0,)), ((), ())), preferred_element_type=jnp.float32
    )


def contract_cols(left, right):
    return lax.dot_general(
        left, right, (((1,), (1,)), ((), ())), preferred_element_type=jnp.float32
    )


def local_terms(block, gate_weight, up_weight, down_weight):
    inputs = block[0]
    weighted = block[1]
    gate = contract_cols(inputs, gate_weight)
    up = contract_cols(inputs, up_weight)
    sig = jax.nn.sigmoid(gate)
    act = gate * sig
    hidden = (act * up).astype(jnp.bfloat16)
    hidden_grad = contract_cols(weighted, down_weight)
    gate_term = (hidden_grad * up * sig * (1.0 + gate * (1.0 - sig))).astype(jnp.bfloat16)
    up_term = (hidden_grad * act).astype(jnp.bfloat16)
    increments = (
        contract_rows(gate_term, inputs),
        contract_rows(up_term, inputs),
        contract_rows(hidden, weighted),
    )
    return (gate_term, up_term, increments)


def visit(block, gate_weight, up_weight, down_weight):
    gate_term, up_term, increments = local_terms(block, gate_weight, up_weight, down_weight)
    partial_sum = jnp.dot(gate_term, gate_weight, preferred_element_type=jnp.float32) + jnp.dot(
        up_term, up_weight, preferred_element_type=jnp.float32
    )
    return (partial_sum, increments)


def add_three(first, second):
    return (first[0] + second[0], first[1] + second[1], first[2] + second[2])


def body(tokens, cotangent, step_lengths, step_labels, gate_weight, up_weight, down_weight):
    rows = tokens.shape[0]
    cycle_size = lax.axis_size("weight")
    steps = step_lengths.shape[1]
    ends = jnp.cumsum(step_lengths[0])
    position = jnp.arange(rows, dtype=jnp.int32)
    segment = jnp.sum((position[:, None] >= ends[None, :]).astype(jnp.int32), axis=1)
    onehot = (segment[:, None] == jnp.arange(steps, dtype=jnp.int32)[None, :]).astype(jnp.float32)
    per_step = (1.0 + 2.0 * step_labels[0].astype(jnp.float32)) * lax.rsqrt(
        step_lengths[0].astype(jnp.float32) * steps / rows
    )
    factor = jnp.sum(onehot * per_step[None, :], axis=1)
    weighted = (cotangent.astype(jnp.float32) * factor[:, None]).astype(jnp.bfloat16)
    stacked = jnp.stack([tokens, weighted])
    own_sum, grads = visit(stacked, gate_weight, up_weight, down_weight)
    block = stacked
    carried = jnp.zeros_like(own_sum)
    for turn in range(1, cycle_size):
        block = shifted(block, "weight", 1)
        term, increments = visit(block, gate_weight, up_weight, down_weight)
        carried = shifted(carried + term, "weight", 1)
        grads = add_three(grads, increments)
    group_grad = own_sum + carried
    input_grad = lax.psum_scatter(group_grad, "dp", scatter_dimension=1, tiled=True)
    total = rows * cycle_size
    scale = 1.0 / total**0.5
    return (input_grad.astype(jnp.bfloat16), grads[0] * scale, grads[1] * scale, grads[2] * scale)


def solution(mesh):
    return jax.shard_map(
        body,
        mesh=mesh,
        in_specs=(
            P("weight", None),
            P("weight", None),
            P("weight", None),
            P("weight", None),
            P(("dp", "weight"), None),
            P(("dp", "weight"), None),
            P(("dp", "weight"), None),
        ),
        out_specs=(
            P("weight", "dp"),
            P(("dp", "weight"), None),
            P(("dp", "weight"), None),
            P(("dp", "weight"), None),
        ),
        check_vma=False,
    )
```

profile of v0, /device:TPU:1, one launch (start us, length us, event | category | flops | bytes accessed | tf_op | source)
XLA Modules:
  0.0 776.6 jit_solution(6893978173049821062)
XLA Ops:
  8.0 0.8 reduce-window.8
  9.0 1.5 fusion.50
  10.7 2.1 collective-permute-start
  12.9 45.8 %collective-permute-done = bf16[2,128,4096]{2,1,0:T(8,128)(2,1)S(1)} collective-permute-done((bf16[2,128,4096]{2,1,0:T(8,128)(2,1)S(1)}, bf16[2,128,4096]{2,1,0:T(8,128)(2,1)S(1)}, u32[]{:S(2)}, u32[]{:S(2)}) %collective-permute-start) | collective-permute-done | bytes 2097184 | tf_op jit(solution)/shard_map/ppermute | solution.py:10
  61.5 2.5 collective-permute-start.1
  64.0 40.6 %collective-permute-done.2 = bf16[2,128,4096]{2,1,0:T(8,128)(2,1)S(1)} collective-permute-done((bf16[2,128,4096]{2,1,0:T(8,128)(2,1)S(1)}, bf16[2,128,4096]{2,1,0:T(8,128)(2,1)S(1)}, u32[]{:S(2)}, u32[]{:S(2)}) %collective-permute-start.2) | collective-permute-done | bytes 2097184 | tf_op jit(solution)/shard_map/ppermute | solution.py:10
  106.8 42.8 %collective-permute-done.1 = f32[128,4096]{1,0:T(8,128)S(1)} collective-permute-done((f32[128,4096]{1,0:T(8,128)S(1)}, f32[128,4096]{1,0:T(8,128)S(1)}, u32[]{:S(2)}, u32[]{:S(2)}) %collective-permute-start.1) | collective-permute-done | bytes 2097184 | tf_op jit(solution)/shard_map/ppermute | solution.py:10
  150.5 44.1 %collective-permute-done.4 = bf16[2,128,4096]{2,1,0:T(8,128)(2,1)S(1)} collective-permute-done((bf16[2,128,4096]{2,1,0:T(8,128)(2,1)S(1)}, bf16[2,128,4096]{2,1,0:T(8,128)(2,1)S(1)}, u32[]{:S(2)}, u32[]{:S(2)}) %collective-permute-start.4) | collective-permute-done | bytes 2097184 | tf_op jit(solution)/shard_map/ppermute | solution.py:10
  197.2 42.3 %collective-permute-done.3 = f32[128,4096]{1,0:T(8,128)S(1)} collective-permute-done((f32[128,4096]{1,0:T(8,128)S(1)}, f32[128,4096]{1,0:T(8,128)S(1)}, u32[]{:S(2)}, u32[]{:S(2)}) %collective-permute-start.3) | collective-permute-done | bytes 2097184 | tf_op jit(solution)/shard_map/ppermute | solution.py:10
  241.0 43.4 %collective-permute-done.6 = bf16[2,128,4096]{2,1,0:T(8,128)(2,1)S(1)} collective-permute-done((bf16[2,128,4096]{2,1,0:T(8,128)(2,1)S(1)}, bf16[2,128,4096]{2,1,0:T(8,128)(2,1)S(1)}, u32[]{:S(2)}, u32[]{:S(2)}) %collective-permute-start.6) | collective-permute-done | bytes 2097184 | tf_op jit(solution)/shard_map/ppermute | solution.py:10
  287.1 42.3 %collective-permute-done.5 = f32[128,4096]{1,0:T(8,128)S(1)} collective-permute-done((f32[128,4096]{1,0:T(8,128)S(1)}, f32[128,4096]{1,0:T(8,128)S(1)}, u32[]{:S(2)}, u32[]{:S(2)}) %collective-permute-start.5) | collective-permute-done | bytes 2097184 | tf_op jit(solution)/shard_map/ppermute | solution.py:10
  331.2 43.1 %collective-permute-done.8 = bf16[2,128,4096]{2,1,0:T(8,128)(2,1)S(1)} collective-permute-done((bf16[2,128,4096]{2,1,0:T(8,128)(2,1)S(1)}, bf16[2,128,4096]{2,1,0:T(8,128)(2,1)S(1)}, u32[]{:S(2)}, u32[]{:S(2)}) %collective-permute-start.8) | collective-permute-done | bytes 2097184 | tf_op jit(solution)/shard_map/ppermute | solution.py:10
  377.0 42.3 %collective-permute-done.7 = f32[128,4096]{1,0:T(8,128)S(1)} collective-permute-done((f32[128,4096]{1,0:T(8,128)S(1)}, f32[128,4096]{1,0:T(8,128)S(1)}, u32[]{:S(2)}, u32[]{:S(2)}) %collective-permute-start.7) | collective-permute-done | bytes 2097184 | tf_op jit(solution)/shard_map/ppermute | solution.py:10
  421.1 43.1 %collective-permute-done.10 = bf16[2,128,4096]{2,1,0:T(8,128)(2,1)S(1)} collective-permute-done((bf16[2,128,4096]{2,1,0:T(8,128)(2,1)S(1)}, bf16[2,128,4096]{2,1,0:T(8,128)(2,1)S(1)}, u32[]{:S(2)}, u32[]{:S(2)}) %collective-permute-start.10) | collective-permute-done | bytes 2097184 | tf_op jit(solution)/shard_map/ppermute | solution.py:10
  466.8 42.3 %collective-permute-done.9 = f32[128,4096]{1,0:T(8,128)S(1)} collective-permute-done((f32[128,4096]{1,0:T(8,128)S(1)}, f32[128,4096]{1,0:T(8,128)S(1)}, u32[]{:S(2)}, u32[]{:S(2)}) %collective-permute-start.9) | collective-permute-done | bytes 2097184 | tf_op jit(solution)/shard_map/ppermute | solution.py:10
  510.9 43.2 %collective-permute-done.12 = bf16[2,128,4096]{2,1,0:T(8,128)(2,1)S(1)} collective-permute-done((bf16[2,128,4096]{2,1,0:T(8,128)(2,1)S(1)}, bf16[2,128,4096]{2,1,0:T(8,128)(2,1)S(1)}, u32[]{:S(2)}, u32[]{:S(2)}) %collective-permute-start.12) | collective-permute-done | bytes 2097184 | tf_op jit(solution)/shard_map/ppermute | solution.py:10
  556.5 42.5 %collective-permute-done.11 = f32[128,4096]{1,0:T(8,128)S(1)} collective-permute-done((f32[128,4096]{1,0:T(8,128)S(1)}, f32[128,4096]{1,0:T(8,128)S(1)}, u32[]{:S(2)}, u32[]{:S(2)}) %collective-permute-start.11) | collective-permute-done | bytes 2097184 | tf_op jit(solution)/shard_map/ppermute | solution.py:10
  600.8 1.3 convolution_add_fusion.26
  602.1 1.3 convolution_add_fusion.12
  603.4 1.3 convolution_add_fusion.18
  604.7 39.8 %collective-permute-done.13 = f32[128,4096]{1,0:T(8,128)S(1)} collective-permute-done((f32[128,4096]{1,0:T(8,128)S(1)}, f32[128,4096]{1,0:T(8,128)S(1)}, u32[]{:S(2)}, u32[]{:S(2)}) %collective-permute-start.13) | collective-permute-done | bytes 2097184 | tf_op jit(solution)/shard_map/ppermute | solution.py:10
  644.4 1.6 add.193
  646.0 1.6 copy-done.4
  647.6 1.6 convolution_add_fusion.25
  649.5 1.3 copy-done.6
  652.0 1.3 copy-done.8
  654.2 1.3 copy-done.10
  655.4 1.3 fusion.2
  656.7 1.3 fusion.3
  658.0 1.3 fusion.1
  659.3 109.1 %reduce-scatter.2.cloned.1.call-done = f32[128,128]{1,0:T(8,128)} async-done(((f32[128,4096]{1,0:T(8,128)}), f32[128,128]{1,0:T(8,128)}) %reduce-scatter.2.cloned.1.call-update) | async-done | bytes 65552 | tf_op jit(solution)/shard_map/reduce_scatter | solution.py:79
  768.3 1.5 convert_element_type.114
  (106 shorter events, 30.9 us)
Async XLA Ops:
  7.2 51.9 %copy-start = (bf16[64,4096]{1,0:T(8,128)(2,1)S(1)}, bf16[64,4096]{1,0:T(8,128)(2,1)}, u32[]{:S(2)}) copy-start(bf16[64,4096]{1,0:T(8,128)(2,1)} %param.11) | copy-start | bytes 1572868
  7.2 3.3 copy-start.2
  7.2 761.1 %reduce-scatter.2.cloned.1.call-start = ((), (), s32[]{:S(2)}) async-start(), calls=%async_computation.1 | async-start | bytes 2162688 | tf_op jit(solution)/shard_map/reduce_scatter | solution.py:79
  10.5 49.1 %copy-start.1 = (bf16[64,4096]{1,0:T(8,128)(2,1)S(1)}, bf16[64,4096]{1,0:T(8,128)(2,1)}, u32[]{:S(2)}) copy-start(bf16[64,4096]{1,0:T(8,128)(2,1)} %param.12) | copy-start | bytes 1572868
  10.7 49.3 %copy-start.14 = (bf16[64,4096]{1,0:T(8,128)(2,1)S(1)}, bf16[64,4096]{1,0:T(8,128)(2,1)}, u32[]{:S(2)}) copy-start(bf16[64,4096]{1,0:T(8,128)(2,1)} %param.13) | copy-start | bytes 1572868
  10.7 47.9 %collective-permute-start = (bf16[2,128,4096]{2,1,0:T(8,128)(2,1)S(1)}, bf16[2,128,4096]{2,1,0:T(8,128)(2,1)S(1)}, u32[]{:S(2)}, u32[]{:S(2)}) collective-permute-start(bf16[2,128,4096]{2,1,0:T(8,128)(2,1)S(1)} %pad_maximum_fusion), channel_id=1, source_target_pairs={{0,1},{1,2},{2,3},{3,4},{4,5},{5,6},{6,7},{7,0},{8,9},{9,10},{10,1... | collective-permute-start | bytes 6291464 | tf_op jit(solution)/shard_map/ppermute | solution.py:10
  58.7 46.0 %collective-permute-start.2 = (bf16[2,128,4096]{2,1,0:T(8,128)(2,1)S(1)}, bf16[2,128,4096]{2,1,0:T(8,128)(2,1)S(1)}, u32[]{:S(2)}, u32[]{:S(2)}) collective-permute-start(bf16[2,128,4096]{2,1,0:T(8,128)(2,1)S(1)} %collective-permute-done), channel_id=1, source_target_pairs={{0,1},{1,2},{2,3},{3,4},{4,5},{5,6},{6,7},{7,0},{8,9},{9,10},{10,1... | collective-permute-start | bytes 6291464 | tf_op jit(solution)/shard_map/ppermute | solution.py:10
  61.5 88.1 %collective-permute-start.1 = (f32[128,4096]{1,0:T(8,128)S(1)}, f32[128,4096]{1,0:T(8,128)S(1)}, u32[]{:S(2)}, u32[]{:S(2)}) collective-permute-start(f32[128,4096]{1,0:T(8,128)S(1)} %convolution_add_fusion.6), channel_id=1, source_target_pairs={{0,1},{1,2},{2,3},{3,4},{4,5},{5,6},{6,7},{7,0},{8,9},{9,10},{10,1... | collective-permute-start | bytes 6291464 | tf_op jit(solution)/shard_map/ppermute | solution.py:10
  104.7 89.9 %collective-permute-start.4 = (bf16[2,128,4096]{2,1,0:T(8,128)(2,1)S(1)}, bf16[2,128,4096]{2,1,0:T(8,128)(2,1)S(1)}, u32[]{:S(2)}, u32[]{:S(2)}) collective-permute-start(bf16[2,128,4096]{2,1,0:T(8,128)(2,1)S(1)} %collective-permute-done.2), channel_id=1, source_target_pairs={{0,1},{1,2},{2,3},{3,4},{4,5},{5,6},{6,7},{7,0},{8,9},{9,10},{10,1... | collective-permute-start | bytes 6291464 | tf_op jit(solution)/shard_map/ppermute | solution.py:10
  150.1 89.3 %collective-permute-start.3 = (f32[128,4096]{1,0:T(8,128)S(1)}, f32[128,4096]{1,0:T(8,128)S(1)}, u32[]{:S(2)}, u32[]{:S(2)}) collective-permute-start(f32[128,4096]{1,0:T(8,128)S(1)} %fusion), channel_id=1, source_target_pairs={{0,1},{1,2},{2,3},{3,4},{4,5},{5,6},{6,7},{7,0},{8,9},{9,10},{10,1... | collective-permute-start | bytes 6291464 | tf_op jit(solution)/shard_map/ppermute | solution.py:10
  194.5 89.9 %collective-permute-start.6 = (bf16[2,128,4096]{2,1,0:T(8,128)(2,1)S(1)}, bf16[2,128,4096]{2,1,0:T(8,128)(2,1)S(1)}, u32[]{:S(2)}, u32[]{:S(2)}) collective-permute-start(bf16[2,128,4096]{2,1,0:T(8,128)(2,1)S(1)} %collective-permute-done.4), channel_id=1, source_target_pairs={{0,1},{1,2},{2,3},{3,4},{4,5},{5,6},{6,7},{7,0},{8,9},{9,10},{10,1... | collective-permute-start | bytes 6291464 | tf_op jit(solution)/shard_map/ppermute | solution.py:10
  239.7 89.6 %collective-permute-start.5 = (f32[128,4096]{1,0:T(8,128)S(1)}, f32[128,4096]{1,0:T(8,128)S(1)}, u32[]{:S(2)}, u32[]{:S(2)}) collective-permute-start(f32[128,4096]{1,0:T(8,128)S(1)} %add.176), channel_id=1, source_target_pairs={{0,1},{1,2},{2,3},{3,4},{4,5},{5,6},{6,7},{7,0},{8,9},{9,10},{10,1... | collective-permute-start | bytes 6291464 | tf_op jit(solution)/shard_map/ppermute | solution.py:10
  284.4 319.0 %copy-start.3 = (bf16[2,128,4096]{2,1,0:T(8,128)(2,1)}, bf16[2,128,4096]{2,1,0:T(8,128)(2,1)S(1)}, u32[]{:S(2)}) copy-start(bf16[2,128,4096]{2,1,0:T(8,128)(2,1)S(1)} %collective-permute-done.6) | copy-start | bytes 6291460
  284.4 89.9 %collective-permute-start.8 = (bf16[2,128,4096]{2,1,0:T(8,128)(2,1)S(1)}, bf16[2,128,4096]{2,1,0:T(8,128)(2,1)S(1)}, u32[]{:S(2)}, u32[]{:S(2)}) collective-permute-start(bf16[2,128,4096]{2,1,0:T(8,128)(2,1)S(1)} %collective-permute-done.6), channel_id=1, source_target_pairs={{0,1},{1,2},{2,3},{3,4},{4,5},{5,6},{6,7},{7,0},{8,9},{9,10},{10,1... | collective-permute-start | bytes 6291464 | tf_op jit(solution)/shard_map/ppermute | solution.py:10
  287.1 42.9 %copy-start.13 = (bf16[128,4096]{1,0:T(8,128)(2,1)S(1)}, bf16[128,4096]{1,0:T(8,128)(2,1)}, u32[]{:S(2)}) copy-start(bf16[128,4096]{1,0:T(8,128)(2,1)} %param.8) | copy-start | bytes 3145732
  329.6 89.6 %collective-permute-start.7 = (f32[128,4096]{1,0:T(8,128)S(1)}, f32[128,4096]{1,0:T(8,128)S(1)}, u32[]{:S(2)}, u32[]{:S(2)}) collective-permute-start(f32[128,4096]{1,0:T(8,128)S(1)} %add.180), channel_id=1, source_target_pairs={{0,1},{1,2},{2,3},{3,4},{4,5},{5,6},{6,7},{7,0},{8,9},{9,10},{10,1... | collective-permute-start | bytes 6291464 | tf_op jit(solution)/shard_map/ppermute | solution.py:10
  374.3 1.7 copy-start.5
  374.3 89.9 %collective-permute-start.10 = (bf16[2,128,4096]{2,1,0:T(8,128)(2,1)S(1)}, bf16[2,128,4096]{2,1,0:T(8,128)(2,1)S(1)}, u32[]{:S(2)}, u32[]{:S(2)}) collective-permute-start(bf16[2,128,4096]{2,1,0:T(8,128)(2,1)S(1)} %collective-permute-done.8), channel_id=1, source_target_pairs={{0,1},{1,2},{2,3},{3,4},{4,5},{5,6},{6,7},{7,0},{8,9},{9,10},{10,1... | collective-permute-start | bytes 6291464 | tf_op jit(solution)/shard_map/ppermute | solution.py:10
  419.5 89.6 %collective-permute-start.9 = (f32[128,4096]{1,0:T(8,128)S(1)}, f32[128,4096]{1,0:T(8,128)S(1)}, u32[]{:S(2)}, u32[]{:S(2)}) collective-permute-start(f32[128,4096]{1,0:T(8,128)S(1)} %add.184), channel_id=1, source_target_pairs={{0,1},{1,2},{2,3},{3,4},{4,5},{5,6},{6,7},{7,0},{8,9},{9,10},{10,1... | collective-permute-start | bytes 6291464 | tf_op jit(solution)/shard_map/ppermute | solution.py:10
  464.2 1.7 copy-start.7
  464.2 89.9 %collective-permute-start.12 = (bf16[2,128,4096]{2,1,0:T(8,128)(2,1)S(1)}, bf16[2,128,4096]{2,1,0:T(8,128)(2,1)S(1)}, u32[]{:S(2)}, u32[]{:S(2)}) collective-permute-start(bf16[2,128,4096]{2,1,0:T(8,128)(2,1)S(1)} %collective-permute-done.10), channel_id=1, source_target_pairs={{0,1},{1,2},{2,3},{3,4},{4,5},{5,6},{6,7},{7,0},{8,9},{9,10},{10,1... | collective-permute-start | bytes 6291464 | tf_op jit(solution)/shard_map/ppermute | solution.py:10
  509.4 89.6 %collective-permute-start.11 = (f32[128,4096]{1,0:T(8,128)S(1)}, f32[128,4096]{1,0:T(8,128)S(1)}, u32[]{:S(2)}, u32[]{:S(2)}) collective-permute-start(f32[128,4096]{1,0:T(8,128)S(1)} %add.188), channel_id=1, source_target_pairs={{0,1},{1,2},{2,3},{3,4},{4,5},{5,6},{6,7},{7,0},{8,9},{9,10},{10,1... | collective-permute-start | bytes 6291464 | tf_op jit(solution)/shard_map/ppermute | solution.py:10
  554.1 1.5 copy-start.9
  599.3 45.1 %collective-permute-start.13 = (f32[128,4096]{1,0:T(8,128)S(1)}, f32[128,4096]{1,0:T(8,128)S(1)}, u32[]{:S(2)}, u32[]{:S(2)}) collective-permute-start(f32[128,4096]{1,0:T(8,128)S(1)} %add.192), channel_id=1, source_target_pairs={{0,1},{1,2},{2,3},{3,4},{4,5},{5,6},{6,7},{7,0},{8,9},{9,10},{10,1... | collective-permute-start | bytes 6291464 | tf_op jit(solution)/shard_map/ppermute | solution.py:10
  646.0 1.6 copy-start.4
  647.6 1.6 copy-start.11
  649.2 1.6 copy-start.6
  649.2 1.8 copy-start.12
  651.7 1.6 copy-start.8
  653.9 1.6 copy-start.10
Sparse Core Ops, SparseCore 0:
  646.1 122.1 reduce-scatter.1
where the time goes:
time: 781 us; the launch traced here: 777 us
  waiting for transfers between devices  707 us (91%)
  matrix products  33.4 us (4%)
  between operations  14.6 us (2%)
  starting transfers between devices  8.62 us (1%)
    ppermute x14, waiting for transfers between devices, shifted(): return lax.ppermute(value, axis, pairs)  597 us
    reduce_scatter x1, waiting for transfers between devices, body(): lax.psum_scatter(group_grad, 'dp', scatter_dimension=1, tiled=True)  109 us
  transfers between devices with their start and end apart: 15, of which 15 were waited for; matrix products, arithmetic and copies ran while one was open for 4% of the time, Pallas kernels for 0%

commit v1 on v0

v1 whole, which is shorter than its diff:
```python
import jax
import jax.numpy as jnp
from jax import lax
from jax.experimental import pallas as pl
from jax.experimental.pallas import tpu as pltpu
from jax.sharding import PartitionSpec as P

MESH = pl.DeviceIdType.MESH
BF = jnp.bfloat16
F32 = jnp.float32
D = 4096
ROWS = 128
KC = 512
NC = 512


def nt(left, right):
    return lax.dot_general(left, right, (((1,), (1,)), ((), ())), preferred_element_type=F32)


def nn(left, right):
    return jnp.dot(left, right, preferred_element_type=F32)


def kernel(
    lens, labs, tok, cot, wg, wu, wd,
    o_dx, o_g, o_u, o_d,
    X, C, CT, W, ACC, TERMS, TT, SEND, OWNZ, RECV, ZSEND, ZRECV, DW,
    PART, R1A, R1B, QA, QB, R2A, R2B, F, R3, OUT,
    in_sem, ysend, yrecv, xsend, xrecv, zsend, zrecv, dsend, drecv,
    gsend, grecv, zgsend, zgrecv, s1send, s1recv, s2send, s2recv, s3send, s3recv, out_sem,
):
    dp = lax.axis_index("dp")
    wt = lax.axis_index("weight")
    z, xh, c = dp // 4, (dp // 2) % 2, dp % 2
    y, xl = wt // 2, wt % 2
    x = xh * 2 + xl

    def at(dx=0, dy=0, dz=0, dc=0):
        xx = (x + dx) % 4
        yy = (y + dy) % 4
        zz = (z + dz) % 8
        cc = (c + dc) % 2
        return (zz * 4 + (xx // 2) * 2 + cc, yy * 2 + xx % 2)

    def remote(src, dst, ssem, rsem, where):
        return pltpu.make_async_remote_copy(
            src_ref=src, dst_ref=dst, send_sem=ssem, recv_sem=rsem,
            device_id=where, device_id_type=MESH,
        )

    barrier = pltpu.get_barrier_semaphore()
    partners = [at(dz=dz, dc=dc) for dz in range(8) for dc in range(2) if dz or dc]
    partners += [at(dy=d) for d in (1, 2, 3)] + [at(dx=d) for d in (1, 2, 3)]
    for who in partners:
        pl.semaphore_signal(barrier, inc=1, device_id=who, device_id_type=MESH)

    row0 = pl.multiple_of((z % 2) * 64 + c * 32, 32)
    loads = [pltpu.make_async_copy(cot.at[pl.ds(row0, 32)], CT, in_sem.at[0])]
    for p in range(2):
        loads.append(pltpu.make_async_copy(tok.at[pl.ds(row0 + 16 * p, 16)], X.at[0, p], in_sem.at[1 + p]))
    for m, ref in enumerate((wg, wu, wd)):
        loads.append(pltpu.make_async_copy(ref, W.at[m, pl.ds(192, 64)], in_sem.at[3 + m]))
    for copy in loads:
        copy.start()

    position = lax.broadcasted_iota(jnp.int32, (32, 128), 0) + row0
    segment = jnp.zeros((32, 128), jnp.int32)
    end = lens[0, 0]
    segment = segment + (position >= end).astype(jnp.int32)
    for k in range(1, 4):
        end = end + lens[0, k]
        segment = segment + (position >= end).astype(jnp.int32)
    length = jnp.zeros((32, 128), jnp.int32)
    label = jnp.zeros((32, 128), jnp.int32)
    for k in range(4):
        length = jnp.where(segment == k, lens[0, k], length)
        label = jnp.where(segment == k, labs[0, k], label)
    factor = (1.0 + 2.0 * label.astype(F32)) * lax.rsqrt(length.astype(F32) * 4 / ROWS)
    loads[0].wait()
    for j in range(D // 128):
        cols = slice(j * 128, (j + 1) * 128)
        value = (CT[:, cols].astype(F32) * factor).astype(BF)
        C[0, 0, :, cols] = value[:16]
        C[0, 1, :, cols] = value[16:]
    for copy in loads[1:]:
        copy.wait()
    pl.semaphore_wait(barrier, len(partners))

    sends = []

    def go(copy):
        copy.start()
        sends.append(copy)
        return copy

    arrays = (X, C)

    def y_piece(a, p, way, hop):
        dy_src = 0 if hop == 0 else (4 - way) % 4
        dy_dst = (dy_src - way) % 4
        k = (0 if way == 1 else 1) * 6 + (a * 2 + p if hop == 0 else 4 + a)
        return remote(
            arrays[a].at[dy_src * 2, p], arrays[a].at[dy_dst * 2, p],
            ysend.at[k], yrecv.at[k], at(dy=way),
        )

    def x_piece(a, p, dy):
        way = 1 if p == 0 else -1
        k = p * 8 + dy * 2 + a
        return remote(
            arrays[a].at[dy * 2, p], arrays[a].at[dy * 2 + 1, p],
            xsend.at[k], xrecv.at[k], at(dx=way),
        )

    def z_weights(m, way):
        src = 192 if way == 1 else 224
        dst = 64 if way == 1 else 96
        k = m * 2 + (0 if way == 1 else 1)
        return remote(
            W.at[m, pl.ds(src, 32)], W.at[m, pl.ds(dst, 32)],
            zsend.at[k], zrecv.at[k], at(dz=way),
        )

    def d_own(m):
        return remote(
            W.at[m, pl.ds(192, 64)], W.at[m, pl.ds(128, 64)],
            dsend.at[m], drecv.at[m], at(dc=1),
        )

    def d_forward(m, way):
        src = 64 if way == 1 else 96
        dst = 0 if way == 1 else 32
        k = 3 + m * 2 + (0 if way == 1 else 1)
        return remote(
            W.at[m, pl.ds(src, 32)], W.at[m, pl.ds(dst, 32)],
            dsend.at[k], drecv.at[k], at(dc=1),
        )

    for a in range(2):
        for i in range(2):
            for way in (1, -1):
                go(y_piece(a, i if way == 1 else 1 - i, way, 0))
            if i == 0:
                go(x_piece(a, 0, 0))
                go(x_piece(a, 1, 0))
        if a == 0:
            for m in range(3):
                for way in (1, -1):
                    go(z_weights(m, way))
    for m in range(3):
        go(d_own(m))

    for a in range(2):
        for i in range(2):
            for way in (1, -1):
                p = i if way == 1 else 1 - i
                y_piece(a, p, way, 0).wait_recv()
                if i == 0:
                    go(y_piece(a, p, way, 1))
                go(x_piece(a, p, 3 if way == 1 else 1))
    for m in range(3):
        for way in (1, -1):
            z_weights(m, way).wait_recv()
            go(d_forward(m, way))
    for a in range(2):
        for way in (1, -1):
            p = 0 if way == 1 else 1
            y_piece(a, p, way, 1).wait_recv()
            go(x_piece(a, p, 2))
    for m in range(3):
        d_own(m).wait_recv()
        for way in (1, -1):
            d_forward(m, way).wait_recv()
    for dy in (0, 3, 1, 2):
        for a in range(2):
            for p in range(2):
                x_piece(a, p, dy).wait_recv()

    ACC[...] = jnp.zeros_like(ACC)

    def step(k, carry):
        cols = pl.ds(pl.multiple_of(k * KC, KC), KC)
        left = X[:, :, :, cols].reshape(256, KC)
        ACC[0] += nt(left, W[0, :, cols])
        ACC[1] += nt(left, W[1, :, cols])
        left = C[:, :, :, cols].reshape(256, KC)
        ACC[2] += nt(left, W[2, :, cols])
        return carry

    lax.fori_loop(0, D // KC, step, 0)
    gate, up, hidden_grad = ACC[0], ACC[1], ACC[2]
    sig = jax.nn.sigmoid(gate)
    act = gate * sig
    hidden = act * up
    gate_term = hidden_grad * up * sig * (1.0 + gate * (1.0 - sig))
    up_term = hidden_grad * act
    TERMS[:, :256] = gate_term.astype(BF)
    TERMS[:, 256:] = up_term.astype(BF)
    TT[0] = gate_term.T.astype(BF)
    TT[1] = up_term.T.astype(BF)
    TT[2] = hidden.T.astype(BF)

    def weight_grads(first, m, cols):
        right = (C if m == 2 else X)[:, :, :, cols].reshape(256, NC)
        return nn(TT[m, pl.ds(first, 128)], right)

    def grad_to_sibling(half, m):
        k = half * 3 + m
        return remote(SEND.at[half, m], RECV.at[half, m], gsend.at[k], grecv.at[k], at(dc=1))

    def grads(half, keep):
        for m in range(3):
            def tile(j, carry):
                cols = pl.ds(pl.multiple_of(j * NC, NC), NC)
                value = weight_grads(half * 128, m, cols)
                SEND[half, m, :, cols] = value[:64].astype(BF)
                keep[m, :, cols] = value[64:]
                return carry

            lax.fori_loop(0, D // NC, tile, 0)
            go(grad_to_sibling(half, m))

    grads(0, OWNZ)

    def dx_tile(k, carry):
        cols = pl.ds(pl.multiple_of(k * 256, 256), 256)
        value = nn(TERMS[:, :256], W[0, :, cols]) + nn(TERMS[:, 256:], W[1, :, cols])
        PART[k // 2, k % 2] = value.astype(BF).reshape(4, 2, 32, 256)
        return carry

    def x_hi(dx):
        return ((x + dx) % 4) // 2

    def s1a(dy):
        return remote(PART.at[pl.ds(0, 4), :, dy], R1A.at[dy - 1], s1send.at[dy - 1], s1recv.at[dy - 1], at(dy=dy))

    def s1b(dx):
        return remote(
            PART.at[pl.ds(4, 4), x_hi(dx), :, dx % 2], R1B.at[dx - 1],
            s1send.at[2 + dx], s1recv.at[2 + dx], at(dx=dx),
        )

    def s2a(dx):
        return remote(QA.at[:, x_hi(dx), dx % 2], R2A.at[dx - 1], s2send.at[dx - 1], s2recv.at[dx - 1], at(dx=dx))

    def s2b(dy):
        return remote(QB.at[:, dy], R2B.at[dy - 1], s2send.at[2 + dy], s2recv.at[2 + dy], at(dy=dy))

    def s3(dz, dc):
        k = dz * 2 + dc
        return remote(
            F.at[(z + dz) % 8, (c + dc) % 2], R3.at[k], s3send.at[k], s3recv.at[k], at(dz=dz, dc=dc),
        )

    lax.fori_loop(0, 8, dx_tile, 0)
    for dy in (2, 1, 3):
        go(s1a(dy))
    lax.fori_loop(8, 16, dx_tile, 0)
    for dx in (2, 1, 3):
        go(s1b(dx))

    def grad_over_z(m, way):
        rows = pl.ds(0 if way == -1 else 32, 32)
        k = m * 2 + (0 if way == -1 else 1)
        return remote(ZSEND.at[m, rows], ZRECV.at[m, rows], zgsend.at[k], zgrecv.at[k], at(dz=way))

    for m in range(3):
        grad_to_sibling(0, m).wait_recv()
        ZSEND[m] = (OWNZ[m] + RECV[0, m].astype(F32)).astype(BF)
        for way in (1, -1):
            go(grad_over_z(m, way))

    grads(1, DW)

    for dy in (1, 3, 2):
        s1a(dy).wait_recv()
    total = PART[0:4, :, 0].astype(F32)
    for i in range(3):
        total = total + R1A[i].astype(F32)
    QA[...] = total.astype(BF)
    for dx in (2, 1, 3):
        go(s2a(dx))
    for dx in (1, 3, 2):
        s1b(dx).wait_recv()
    total = PART[pl.ds(4, 4), xh, :, 0].astype(F32)
    for i in range(3):
        total = total + R1B[i].astype(F32)
    QB[...] = total.astype(BF)
    for dy in (2, 1, 3):
        go(s2b(dy))

    for m in range(3):
        grad_to_sibling(1, m).wait_recv()
        DW[m] = DW[m] + RECV[1, m].astype(F32)

    for dx in (1, 3, 2):
        s2a(dx).wait_recv()
    total = QA[:, xh, 0].astype(F32)
    for i in range(3):
        total = total + R2A[i].astype(F32)
    F[0:4, 0] = total[:, :, :128].astype(BF)
    F[0:4, 1] = total[:, :, 128:].astype(BF)
    for dy in (1, 3, 2):
        s2b(dy).wait_recv()
    total = QB[:, 0].astype(F32)
    for i in range(3):
        total = total + R2B[i].astype(F32)
    F[4:8, 0] = total[:, :, :128].astype(BF)
    F[4:8, 1] = total[:, :, 128:].astype(BF)
    for dz in (4, 3, 5, 2, 6, 1, 7, 0):
        for dc in range(2):
            if dz or dc:
                go(s3(dz, dc))

    outs = []
    for m, ref in enumerate((o_g, o_u, o_d)):
        for way in (1, -1):
            grad_over_z(m, way).wait_recv()
        DW[m] = (DW[m] + ZRECV[m].astype(F32)) * (1.0 / 32.0)
        copy = pltpu.make_async_copy(DW.at[m], ref, out_sem.at[m])
        copy.start()
        outs.append(copy)

    for dz in range(8):
        for dc in range(2):
            if dz or dc:
                s3(dz, dc).wait_recv()
    for odd in range(2):
        for dc in range(2):
            total = None
            for dz in range(odd, 8, 2):
                if dz == 0 and dc == 0:
                    term = F[z, c].astype(F32)
                else:
                    term = R3[dz * 2 + dc].astype(F32)
                total = term if total is None else total + term
            row = pl.multiple_of(((z + odd) % 2) * 64 + ((c + dc) % 2) * 32, 32)
            OUT[pl.ds(row, 32), :] = total.astype(BF)
    copy = pltpu.make_async_copy(OUT, o_dx, out_sem.at[3])
    copy.start()
    outs.append(copy)
    for copy in outs:
        copy.wait()
    for copy in sends:
        copy.wait_send()


def body(tokens, cotangent, step_lengths, step_labels, gate_weight, up_weight, down_weight):
    dma = pltpu.SemaphoreType.DMA
    any_ = pl.BlockSpec(memory_space=pl.ANY)
    smem = pl.BlockSpec(memory_space=pltpu.SMEM)
    grad = jax.ShapeDtypeStruct((64, D), F32)
    return pl.pallas_call(
        kernel,
        name="ffn_backward",
        out_shape=(jax.ShapeDtypeStruct((128, 128), BF), grad, grad, grad),
        in_specs=[smem, smem] + [any_] * 5,
        out_specs=[any_] * 4,
        scratch_shapes=[
            pltpu.VMEM((8, 2, 16, D), BF),
            pltpu.VMEM((8, 2, 16, D), BF),
            pltpu.VMEM((32, D), BF),
            pltpu.VMEM((3, 256, D), BF),
            pltpu.VMEM((3, 256, 256), F32),
            pltpu.VMEM((256, 512), BF),
            pltpu.VMEM((3, 256, 256), BF),
            pltpu.VMEM((2, 3, 64, D), BF),
            pltpu.VMEM((3, 64, D), F32),
            pltpu.VMEM((2, 3, 64, D), BF),
            pltpu.VMEM((3, 64, D), BF),
            pltpu.VMEM((3, 64, D), BF),
            pltpu.VMEM((3, 64, D), F32),
            pltpu.VMEM((8, 2, 4, 2, 32, 256), BF),
            pltpu.VMEM((3, 4, 2, 2, 32, 256), BF),
            pltpu.VMEM((3, 4, 4, 32, 256), BF),
            pltpu.VMEM((4, 2, 2, 32, 256), BF),
            pltpu.VMEM((4, 4, 32, 256), BF),
            pltpu.VMEM((3, 4, 32, 256), BF),
            pltpu.VMEM((3, 4, 32, 256), BF),
            pltpu.VMEM((8, 2, 32, 128), BF),
            pltpu.VMEM((16, 32, 128), BF),
            pltpu.VMEM((128, 128), BF),
            dma((6,)), dma((12,)), dma((12,)), dma((16,)), dma((16,)),
            dma((6,)), dma((6,)), dma((9,)), dma((9,)),
            dma((6,)), dma((6,)), dma((6,)), dma((6,)),
            dma((6,)), dma((6,)), dma((6,)), dma((6,)), dma((16,)), dma((16,)),
            dma((4,)),
        ],
        compiler_params=pltpu.CompilerParams(
            collective_id=0, has_side_effects=True, vmem_limit_bytes=56 * 2**20
        ),
        cost_estimate=pl.CostEstimate(flops=4_300_000_000, bytes_accessed=8_000_000, transcendentals=65536),
    )(step_lengths, step_labels, tokens, cotangent, gate_weight, up_weight, down_weight)


def solution(mesh):
    return jax.shard_map(
        body,
        mesh=mesh,
        in_specs=(
            P("weight", None),
            P("weight", None),
            P("weight", None),
            P("weight", None),
            P(("dp", "weight"), None),
            P(("dp", "weight"), None),
            P(("dp", "weight"), None),
        ),
        out_specs=(
            P("weight", "dp"),
            P(("dp", "weight"), None),
            P(("dp", "weight"), None),
            P(("dp", "weight"), None),
        ),
        check_vma=False,
    )
```

time: 781 us -> 83.1 us (0.11)
  waiting for transfers between devices: 707 us -> 0 us
  Pallas kernels: 0 us -> 75.9 us
  matrix products: 33.4 us -> 0 us
  between operations: 14.6 us -> 0.64 us
  starting transfers between devices: 8.62 us -> 0 us
    ppermute x14 -> x0, waiting for transfers between devices: 597 us -> none  [shifted(): return lax.ppermute(value, axis, pairs)]
    reduce_scatter x1 -> x0, waiting for transfers between devices: 109 us -> none  [body(): lax.psum_scatter(group_grad, 'dp', scatter_dimension=1, tiled=True)]
    pallas_call x0 -> x1, Pallas kernels: none -> 75.9 us  [body(): pl.pallas_call(kernel, name='ffn_backward', out_shape=(jax.ShapeDtypeStru...]
    dot_general x64 -> x0, matrix products: 33.4 us -> none  [the longest x24 14.4 us: contract_rows(): lax.dot_general(left, right, (((0,), (0,)), ((), ())), preferred_element_...]
    ppermute x14 -> x0, starting transfers between devices: 8.58 us -> none  [shifted(): return lax.ppermute(value, axis, pairs)]
  transfers between devices with their start and end apart: 15 -> 0, of which waited for: 15 -> 0; matrix products, arithmetic and copies ran while one was open for 4% -> 0% of each run, Pallas kernels for 0% -> 0%
where the time goes in v1:
time: 83.1 us; the launch traced here: 82.9 us
  Pallas kernels  75.9 us (91%)
  local copies, waits for them, and re-layouts  6.31 us (8%)
    pallas_call x1, Pallas kernels, body(): pl.pallas_call(kernel, name='ffn_backward', out_shape=(jax.ShapeDtypeStru...  75.9 us
    unnamed x8, local copies, waits for them, and re-layouts  6.31 us

profile of v1, /device:TPU:1, one launch (start us, length us, event | category | flops | bytes accessed | tf_op | source)
XLA Modules:
  0.0 82.9 jit_solution(17221632030763438238)
XLA Ops:
  0.6 75.9 %ffn_backward.1 = (bf16[128,128]{1,0:T(8,128)(2,1)}, f32[64,4096]{1,0:T(8,128)}, f32[64,4096]{1,0:T(8,128)}, f32[64,4096]{1,0:T(8,128)}) custom-call(s32[1,4]{1,0:T(1,128)} %lens.1, s32[1,4]{1,0:T(1,128)} %labs.1, bf16[128,4096]{1,0:T(8,128)(2,1)} %tok.1, bf16[128,4096]{1,0:T(8,128)(2,1)} %cot.1, bf16[64,4096]{1,0:T(8,128)(2,1)} %wg.1, bf16[64,4096]{1,0:T(8,128)(2,1)} %wu.1, ...), custom_call_target="tpu_custom_call" | custom-call | flops 4300000256 | bytes 8000000 | tf_op jit(solution)/shard_map/ffn_backward/pallas_call | solution.py:354
  76.6 1.4 %copy.15 = bf16[128,128]{1,0:T(8,128)(2,1)} copy(bf16[128,128]{1,0:T(8,128)(2,1)} %get-tuple-element.8) | data formatting | bytes 65536
  77.9 0.0 copy-start.1
  77.9 2.4 %copy.16 = f32[64,4096]{1,0:T(8,128)} copy(f32[64,4096]{1,0:T(8,128)} %get-tuple-element.9) | data formatting | bytes 2097152
  80.3 0.0 copy-done.1
  80.3 0.0 copy-start
  80.3 1.0 %copy.17 = f32[64,4096]{1,0:T(8,128)} copy(f32[64,4096]{1,0:T(8,128)S(1)} %copy-done.1) | data formatting | bytes 2097152
  81.3 0.6 copy-done
  81.9 1.0 %copy.18 = f32[64,4096]{1,0:T(8,128)} copy(f32[64,4096]{1,0:T(8,128)S(1)} %copy-done) | data formatting | bytes 2097152
Async XLA Ops:
  77.9 2.4 %copy-start.1 = (f32[64,4096]{1,0:T(8,128)S(1)}, f32[64,4096]{1,0:T(8,128)}, u32[]{:S(2)}) copy-start(f32[64,4096]{1,0:T(8,128)} %get-tuple-element.10) | copy-start | bytes 3145732
  80.3 1.6 %copy-start = (f32[64,4096]{1,0:T(8,128)S(1)}, f32[64,4096]{1,0:T(8,128)}, u32[]{:S(2)}) copy-start(f32[64,4096]{1,0:T(8,128)} %get-tuple-element.11) | copy-start | bytes 3145732

commit v2 on v1

v2 whole, which is shorter than its diff:
```python
import jax
import jax.numpy as jnp
from jax import lax
from jax.experimental import pallas as pl
from jax.experimental.pallas import tpu as pltpu
from jax.sharding import PartitionSpec as P

MESH = pl.DeviceIdType.MESH
BF = jnp.bfloat16
F32 = jnp.float32
D = 4096
ROWS = 128
KC = 512
NC = 512


def nt(left, right):
    return lax.dot_general(left, right, (((1,), (1,)), ((), ())), preferred_element_type=F32)


def nn(left, right):
    return jnp.dot(left, right, preferred_element_type=F32)


def kernel(
    lens, labs, tok, cot, wg, wu, wd,
    o_dx, o_g, o_u, o_d,
    X, C, CT, W, ACC, TERMS, TT, SEND, OWNZ, RECV, ZSEND, ZRECV,
    PART, TA, TB, RA, RB, QA, QB, R2A, R2B, F, R3,
    in_sem, ysend, yrecv, xsend, xrecv, zsend, zrecv, dsend, drecv,
    gsend, grecv, zgsend, zgrecv, s1send, s1recv, s2send, s2recv, s3send, s3recv,
):
    dp = lax.axis_index("dp")
    wt = lax.axis_index("weight")
    z, xh, c = dp // 4, (dp // 2) % 2, dp % 2
    y, xl = wt // 2, wt % 2
    x = xh * 2 + xl

    def at(dx=0, dy=0, dz=0, dc=0):
        xx = (x + dx) % 4
        yy = (y + dy) % 4
        zz = (z + dz) % 8
        cc = (c + dc) % 2
        return (zz * 4 + (xx // 2) * 2 + cc, yy * 2 + xx % 2)

    def remote(src, dst, ssem, rsem, k, where):
        return pltpu.make_async_remote_copy(
            src_ref=src, dst_ref=dst, send_sem=ssem.at[k], recv_sem=rsem.at[k],
            device_id=where, device_id_type=MESH,
        )

    sends = []

    def go(copy):
        copy.start()
        sends.append(copy)
        return copy

    barrier = pltpu.get_barrier_semaphore()
    partners = [at(dz=dz, dc=dc) for dz in range(8) for dc in range(2) if dz or dc]
    partners += [at(dy=d) for d in (1, 2, 3)] + [at(dx=d) for d in (1, 2, 3)]
    for who in partners:
        pl.semaphore_signal(barrier, inc=1, device_id=who, device_id_type=MESH)

    row0 = pl.multiple_of((z % 2) * 64 + c * 32, 32)
    loads = [pltpu.make_async_copy(cot.at[pl.ds(row0, 32)], CT, in_sem.at[0])]
    for p in range(2):
        loads.append(pltpu.make_async_copy(tok.at[pl.ds(row0 + 16 * p, 16)], X.at[0, p], in_sem.at[1 + p]))
    for m, ref in enumerate((wg, wu, wd)):
        loads.append(pltpu.make_async_copy(ref, W.at[m, pl.ds(192, 64)], in_sem.at[3 + m]))
    for copy in loads:
        copy.start()

    position = lax.broadcasted_iota(jnp.int32, (32, 128), 0) + row0
    segment = jnp.zeros((32, 128), jnp.int32)
    end = lens[0, 0]
    segment = segment + (position >= end).astype(jnp.int32)
    for k in range(1, 4):
        end = end + lens[0, k]
        segment = segment + (position >= end).astype(jnp.int32)
    length = jnp.zeros((32, 128), jnp.int32)
    label = jnp.zeros((32, 128), jnp.int32)
    for k in range(4):
        length = jnp.where(segment == k, lens[0, k], length)
        label = jnp.where(segment == k, labs[0, k], label)
    factor = (1.0 + 2.0 * label.astype(F32)) * lax.rsqrt(length.astype(F32) * 4 / ROWS)
    loads[0].wait()
    for j in range(D // 128):
        cols = slice(j * 128, (j + 1) * 128)
        value = (CT[:, cols].astype(F32) * factor).astype(BF)
        C[0, 0, :, cols] = value[:16]
        C[0, 1, :, cols] = value[16:]
    for copy in loads[1:]:
        copy.wait()
    pl.semaphore_wait(barrier, len(partners))

    arrays = (X, C)

    def first(way):
        return 0 if way == 1 else 1

    def side(way):
        return 3 if way == 1 else 1

    def y_piece(a, p, way):
        k = first(way) * 8 + a * 2 + p
        return remote(arrays[a].at[0, p], arrays[a].at[side(way) * 2, p], ysend, yrecv, k, at(dy=way))

    def y_next(a, way):
        p = first(way)
        k = first(way) * 8 + 4 + a
        return remote(arrays[a].at[side(way) * 2, p], arrays[a].at[4, p], ysend, yrecv, k, at(dy=way))

    def y_other(way):
        p = first(way)
        k = first(way) * 8 + 6
        return remote(C.at[side(way) * 2 + 1, p], C.at[5, p], ysend, yrecv, k, at(dy=way))

    def x_piece(a, p, dy):
        k = p * 8 + dy * 2 + a
        return remote(
            arrays[a].at[dy * 2, p], arrays[a].at[dy * 2 + 1, p], xsend, xrecv, k, at(dx=1 if p == 0 else -1)
        )

    def z_weights(m, way):
        rows = (192, 64) if way == 1 else (224, 96)
        return remote(
            W.at[m, pl.ds(rows[0], 32)], W.at[m, pl.ds(rows[1], 32)],
            zsend, zrecv, m * 2 + first(way), at(dz=way),
        )

    def d_own(m):
        return remote(W.at[m, pl.ds(192, 64)], W.at[m, pl.ds(128, 64)], dsend, drecv, m, at(dc=1))

    def d_forward(m):
        return remote(W.at[m, pl.ds(64, 64)], W.at[m, pl.ds(0, 64)], dsend, drecv, 3 + m, at(dc=1))

    both = (1, -1)

    def weights_on(m):
        for way in both:
            z_weights(m, way).wait_recv()
        go(d_forward(m))

    for way in both:
        go(y_piece(0, first(way), way))
    for p in range(2):
        go(x_piece(0, p, 0))
    for way in both:
        go(z_weights(0, way))
    for way in both:
        go(y_piece(0, 1 - first(way), way))
    for p in range(2):
        go(x_piece(1, p, 0))
    for way in both:
        go(y_piece(1, first(way), way))
    for m in (1, 2):
        for way in both:
            go(z_weights(m, way))
    for m in range(3):
        go(d_own(m))
    for way in both:
        y_piece(0, first(way), way).wait_recv()
        go(y_next(0, way))
        go(x_piece(0, first(way), side(way)))
    for way in both:
        go(y_piece(1, 1 - first(way), way))
    for way in both:
        y_piece(0, 1 - first(way), way).wait_recv()
        go(x_piece(0, 1 - first(way), side(way)))
    weights_on(0)
    for way in both:
        y_piece(1, first(way), way).wait_recv()
        go(y_next(1, way))
        go(x_piece(1, first(way), side(way)))
    for way in both:
        y_next(0, way).wait_recv()
        go(x_piece(0, first(way), 2))
    weights_on(1)
    for way in both:
        y_piece(1, 1 - first(way), way).wait_recv()
        go(x_piece(1, 1 - first(way), side(way)))
    for way in both:
        x_piece(1, first(way), side(way)).wait_recv()
        go(y_other(way))
    for m in range(2):
        d_own(m).wait_recv()
        d_forward(m).wait_recv()
    for dy in (0, 3, 1, 2):
        for p in range(2):
            x_piece(0, p, dy).wait_recv()

    def contract(m, a):
        ACC[m] = jnp.zeros((256, 256), F32)

        def step(k, carry):
            cols = pl.ds(pl.multiple_of(k * KC, KC), KC)
            ACC[m] += nt(arrays[a][:, :, :, cols].reshape(256, KC), W[m, :, cols])
            return carry

        lax.fori_loop(0, D // KC, step, 0)

    contract(0, 0)
    contract(1, 0)
    weights_on(2)
    gate, up = ACC[0], ACC[1]
    sig = jax.nn.sigmoid(gate)
    act = gate * sig
    TT[2] = (act * up).T.astype(BF)

    for way in both:
        y_next(1, way).wait_recv()
    for way in both:
        x_piece(1, 1 - first(way), side(way)).wait_recv()
    for p in range(2):
        x_piece(1, p, 0).wait_recv()
    for way in both:
        y_other(way).wait_recv()

    outs = (o_g, o_u, o_d)

    def grad_to_sibling(half, m):
        return remote(SEND.at[half, m], RECV.at[half, m], gsend, grecv, half * 3 + m, at(dc=1))

    def grads(half, m):
        def tile(j, carry):
            cols = pl.ds(pl.multiple_of(j * NC, NC), NC)
            right = arrays[m // 2][:, :, :, cols].reshape(256, NC)
            value = nn(TT[m, pl.ds(half * 128, 128)], right)
            SEND[half, m, :, cols] = value[:64].astype(BF)
            if half:
                outs[m][:, cols] = value[64:]
            else:
                OWNZ[m, :, cols] = value[64:]
            return carry

        lax.fori_loop(0, D // NC, tile, 0)
        go(grad_to_sibling(half, m))

    def grad_over_z(m, way):
        rows = pl.ds(0 if way == -1 else 32, 32)
        return remote(ZSEND.at[m, rows], ZRECV.at[m, rows], zgsend, zgrecv, m * 2 + first(way), at(dz=way))

    def grads_over_z(m):
        grad_to_sibling(0, m).wait_recv()
        ZSEND[m] = (OWNZ[m] + RECV[0, m].astype(F32)).astype(BF)
        for way in both:
            go(grad_over_z(m, way))

    grads(0, 2)

    d_own(2).wait_recv()
    d_forward(2).wait_recv()
    contract(2, 1)
    hidden_grad = ACC[2]
    gate, up = ACC[0], ACC[1]
    sig = jax.nn.sigmoid(gate)
    act = gate * sig
    gate_term = hidden_grad * up * sig * (1.0 + gate * (1.0 - sig))
    up_term = hidden_grad * act
    TERMS[:, :256] = gate_term.astype(BF)
    TERMS[:, 256:] = up_term.astype(BF)
    TT[0] = gate_term.T.astype(BF)
    TT[1] = up_term.T.astype(BF)

    def dx_tile(k, carry):
        cols = pl.ds(pl.multiple_of(k * 256, 256), 256)
        value = nn(TERMS[:, :256], W[0, :, cols]) + nn(TERMS[:, 256:], W[1, :, cols])
        PART[k // 2, k % 2] = value.astype(BF).reshape(4, 2, 32, 256)
        return carry

    def x_hi(dx):
        return ((x + dx) % 4) // 2

    def half_a(h, dy):
        return PART.at[pl.ds(h * 2, 2), :, dy]

    def half_b(h, dx):
        return PART.at[pl.ds(4 + h * 2, 2), x_hi(dx), :, dx % 2]

    def s1_opposite(b, way):
        h = first(way)
        src, where = (half_b(h, 2), at(dx=way)) if b else (half_a(h, 2), at(dy=way))
        return remote(src, (TB if b else TA).at[h], s1send, s1recv, b * 6 + h, where)

    def s1_direct(b, way):
        i, near = first(way), way % 4
        src, where = (half_b(1 - i, near), at(dx=way)) if b else (half_a(1 - i, near), at(dy=way))
        return remote(src, (RB if b else RA).at[i], s1send, s1recv, b * 6 + 2 + i, where)

    def s1_summed(b, way):
        i, near = first(way), way % 4
        src, where = (half_b(i, near), at(dx=way)) if b else (half_a(i, near), at(dy=way))
        return remote(src, (RB if b else RA).at[2 + i], s1send, s1recv, b * 6 + 4 + i, where)

    def s1_sum(b, way):
        h, near = first(way), way % 4
        s1_opposite(b, way).wait_recv()
        mine = half_b(h, near) if b else half_a(h, near)
        mine[...] = (mine[...].astype(F32) + (TB if b else TA)[h].astype(F32)).astype(BF)
        go(s1_summed(b, way))

    def s2a(dx):
        return remote(QA.at[:, x_hi(dx), dx % 2], R2A.at[dx - 1], s2send, s2recv, dx - 1, at(dx=dx))

    def s2b(dy):
        return remote(QB.at[:, dy], R2B.at[dy - 1], s2send, s2recv, 2 + dy, at(dy=dy))

    def s3(dz, dc):
        k = dz * 2 + dc
        return remote(
            F.at[(z + dz) % 8, (c + dc) % 2], R3.at[k], s3send, s3recv, k, at(dz=dz, dc=dc)
        )

    for b in range(2):
        lax.fori_loop(b * 8, b * 8 + 8, dx_tile, 0)
        for way in both:
            go(s1_opposite(b, way))
        for way in both:
            go(s1_direct(b, way))
        if b == 0:
            grads_over_z(2)
    grads(0, 0)
    for way in both:
        s1_sum(0, way)
    grads(0, 1)
    for way in both:
        s1_sum(1, way)
    grads_over_z(0)
    grads_over_z(1)
    for m in (2, 0, 1):
        grads(1, m)

    def s1_total(b):
        for way in both:
            s1_direct(b, way).wait_recv()
        for way in both:
            s1_summed(b, way).wait_recv()
        came = RB if b else RA
        for h in range(2):
            own = half_b(h, 0) if b else half_a(h, 0)
            total = own[...].astype(F32) + came[1 - h].astype(F32) + came[2 + h].astype(F32)
            if b:
                QB[h * 2 : h * 2 + 2] = total.astype(BF)
            else:
                QA[h * 2 : h * 2 + 2] = total.astype(BF)

    s1_total(0)
    for dx in (2, 1, 3):
        go(s2a(dx))
    s1_total(1)
    for dy in (2, 1, 3):
        go(s2b(dy))

    for m in (2, 0, 1):
        grad_to_sibling(1, m).wait_recv()
        outs[m][...] += RECV[1, m].astype(F32)

    for dx in (1, 3, 2):
        s2a(dx).wait_recv()
    total = QA[:, xh, 0].astype(F32)
    for i in range(3):
        total = total + R2A[i].astype(F32)
    F[0:4, 0] = total[:, :, :128].astype(BF)
    F[0:4, 1] = total[:, :, 128:].astype(BF)
    for dy in (1, 3, 2):
        s2b(dy).wait_recv()
    total = QB[:, 0].astype(F32)
    for i in range(3):
        total = total + R2B[i].astype(F32)
    F[4:8, 0] = total[:, :, :128].astype(BF)
    F[4:8, 1] = total[:, :, 128:].astype(BF)
    for dz in (4, 3, 5, 2, 6, 1, 7, 0):
        for dc in range(2):
            if dz or dc:
                go(s3(dz, dc))

    def finish(m):
        for way in both:
            grad_over_z(m, way).wait_recv()
        outs[m][...] = (outs[m][...] + ZRECV[m].astype(F32)) * (1.0 / 32.0)

    finish(2)
    finish(0)
    for dz in range(8):
        for dc in range(2):
            if dz or dc:
                s3(dz, dc).wait_recv()
    for odd in range(2):
        for dc in range(2):
            total = None
            for dz in range(odd, 8, 2):
                if dz == 0 and dc == 0:
                    term = F[z, c].astype(F32)
                else:
                    term = R3[dz * 2 + dc].astype(F32)
                total = term if total is None else total + term
            row = pl.multiple_of(((z + odd) % 2) * 64 + ((c + dc) % 2) * 32, 32)
            o_dx[pl.ds(row, 32), :] = total.astype(BF)
    finish(1)
    for copy in sends:
        copy.wait_send()


def write_out(dx, g, u, d, o_dx, o_g, o_u, o_d, sem):
    copies = [
        pltpu.make_async_copy(src, dst, sem.at[k])
        for k, (src, dst) in enumerate(((g, o_g), (u, o_u), (d, o_d), (dx, o_dx)))
    ]
    for copy in copies:
        copy.start()
    for copy in copies:
        copy.wait()


def body(tokens, cotangent, step_lengths, step_labels, gate_weight, up_weight, down_weight):
    dma = pltpu.SemaphoreType.DMA
    hbm = pl.BlockSpec(memory_space=pltpu.HBM)
    smem = pl.BlockSpec(memory_space=pltpu.SMEM)
    vmem = pl.BlockSpec(memory_space=pltpu.VMEM)
    shapes = [((128, 128), BF)] + [((64, D), F32)] * 3
    held = pl.pallas_call(
        kernel,
        name="ffn_backward",
        out_shape=tuple(pltpu.VMEM(shape, dtype) for shape, dtype in shapes),
        in_specs=[smem, smem] + [hbm] * 5,
        out_specs=[vmem] * 4,
        scratch_shapes=[
            pltpu.VMEM((8, 2, 16, D), BF),
            pltpu.VMEM((8, 2, 16, D), BF),
            pltpu.VMEM((32, D), BF),
            pltpu.VMEM((3, 256, D), BF),
            pltpu.VMEM((3, 256, 256), F32),
            pltpu.VMEM((256, 512), BF),
            pltpu.VMEM((3, 256, 256), BF),
            pltpu.VMEM((2, 3, 64, D), BF),
            pltpu.VMEM((3, 64, D), F32),
            pltpu.VMEM((2, 3, 64, D), BF),
            pltpu.VMEM((3, 64, D), BF),
            pltpu.VMEM((3, 64, D), BF),
            pltpu.VMEM((8, 2, 4, 2, 32, 256), BF),
            pltpu.VMEM((2, 2, 2, 2, 32, 256), BF),
            pltpu.VMEM((2, 2, 4, 32, 256), BF),
            pltpu.VMEM((4, 2, 2, 2, 32, 256), BF),
            pltpu.VMEM((4, 2, 4, 32, 256), BF),
            pltpu.VMEM((4, 2, 2, 32, 256), BF),
            pltpu.VMEM((4, 4, 32, 256), BF),
            pltpu.VMEM((3, 4, 32, 256), BF),
            pltpu.VMEM((3, 4, 32, 256), BF),
            pltpu.VMEM((8, 2, 32, 128), BF),
            pltpu.VMEM((16, 32, 128), BF),
            dma((6,)), dma((16,)), dma((16,)), dma((16,)), dma((16,)),
            dma((6,)), dma((6,)), dma((6,)), dma((6,)),
            dma((6,)), dma((6,)), dma((6,)), dma((6,)),
            dma((12,)), dma((12,)), dma((6,)), dma((6,)), dma((16,)), dma((16,)),
        ],
        compiler_params=pltpu.CompilerParams(
            collective_id=0, has_side_effects=True, vmem_limit_bytes=60 * 2**20 + 2**19
        ),
        cost_estimate=pl.CostEstimate(flops=4_300_000_000, bytes_accessed=8_000_000, transcendentals=65536),
    )(step_lengths, step_labels, tokens, cotangent, gate_weight, up_weight, down_weight)
    return pl.pallas_call(
        write_out,
        name="write_out",
        out_shape=tuple(jax.ShapeDtypeStruct(shape, dtype) for shape, dtype in shapes),
        in_specs=[vmem] * 4,
        out_specs=[hbm] * 4,
        scratch_shapes=[dma((4,))],
    )(*held)


def solution(mesh):
    return jax.shard_map(
        body,
        mesh=mesh,
        in_specs=(
            P("weight", None),
            P("weight", None),
            P("weight", None),
            P("weight", None),
            P(("dp", "weight"), None),
            P(("dp", "weight"), None),
            P(("dp", "weight"), None),
        ),
        out_specs=(
            P("weight", "dp"),
            P(("dp", "weight"), None),
            P(("dp", "weight"), None),
            P(("dp", "weight"), None),
        ),
        check_vma=False,
    )
```

time: 83.1 us -> 75.6 us (0.910)
  Pallas kernels: 75.9 us -> 71.3 us
  local copies, waits for them, and re-layouts: 6.31 us -> 3.57 us
    pallas_call x1 -> x2, Pallas kernels: 75.9 us -> 71.3 us  [the longest x1 67.7 us: body(): pl.pallas_call(kernel, name='ffn_backward', out_shape=tuple((pltpu.VMEM(s...]
    unnamed x8, local copies, waits for them, and re-layouts: 6.31 us -> 3.57 us
where the time goes in v2:
time: 75.6 us; the launch traced here: 75.5 us
  Pallas kernels  71.3 us (94%)
  local copies, waits for them, and re-layouts  3.57 us (5%)
    pallas_call x1, Pallas kernels, body(): pl.pallas_call(kernel, name='ffn_backward', out_shape=tuple((pltpu.VMEM(s...  67.7 us
    unnamed x8, local copies, waits for them, and re-layouts  3.57 us
    pallas_call x1, Pallas kernels, body(): pl.pallas_call(write_out, name='write_out', out_shape=tuple((jax.ShapeDty...  3.57 us

profile of v2, /device:TPU:1, one launch (start us, length us, event | category | flops | bytes accessed | tf_op | source)
XLA Modules:
  0.0 75.5 jit_solution(11680750603684273243)
XLA Ops:
  0.6 67.7 %ffn_backward.1 = (bf16[128,128]{1,0:T(8,128)(2,1)S(1)}, f32[64,4096]{1,0:T(8,128)S(1)}, f32[64,4096]{1,0:T(8,128)S(1)}, f32[64,4096]{1,0:T(8,128)S(1)}) custom-call(s32[1,4]{1,0:T(1,128)} %lens.1, s32[1,4]{1,0:T(1,128)} %labs.1, bf16[128,4096]{1,0:T(8,128)(2,1)} %tok.1, bf16[128,4096]{1,0:T(8,128)(2,1)} %cot.1, bf16[64,4096]{1,0:T(8,128)(2,1)} %wg.1, ...), custom_call_target="tpu_custom_call" | custom-call | flops 4300000256 | bytes 8000000 | tf_op jit(solution)/shard_map/ffn_backward/pallas_call | solution.py:422
  68.3 0.0 copy-start
  68.3 1.0 %copy-done = f32[64,4096]{1,0:T(8,128)} copy-done((f32[64,4096]{1,0:T(8,128)}, f32[64,4096]{1,0:T(8,128)S(1)}, u32[]{:S(2)}) %copy-start) | copy-done | bytes 1048600
  69.3 0.0 copy-start.1
  69.3 1.0 %copy-done.1 = f32[64,4096]{1,0:T(8,128)} copy-done((f32[64,4096]{1,0:T(8,128)}, f32[64,4096]{1,0:T(8,128)S(1)}, u32[]{:S(2)}) %copy-start.1) | copy-done | bytes 1048600
  70.3 0.0 copy-start.2
  70.3 1.0 %copy-done.2 = f32[64,4096]{1,0:T(8,128)} copy-done((f32[64,4096]{1,0:T(8,128)}, f32[64,4096]{1,0:T(8,128)S(1)}, u32[]{:S(2)}) %copy-start.2) | copy-done | bytes 1048600
  71.3 0.0 copy-start.3
  71.3 0.6 copy-done.3
  71.9 3.6 %write_out.1 = (bf16[128,128]{1,0:T(8,128)(2,1)}, f32[64,4096]{1,0:T(8,128)}, f32[64,4096]{1,0:T(8,128)}, f32[64,4096]{1,0:T(8,128)}) custom-call(bf16[128,128]{1,0:T(8,128)(2,1)} %copy-done.3, f32[64,4096]{1,0:T(8,128)} %copy-done, f32[64,4096]{1,0:T(8,128)} %copy-done.1, f32[64,4096]{1,0:T(8,128)} %copy-done.2), custom_call_target="tpu_custom_call" | custom-call | tf_op jit(solution)/shard_map/write_out/pallas_call | solution.py:462
Async XLA Ops:
  68.3 1.0 %copy-start = (f32[64,4096]{1,0:T(8,128)}, f32[64,4096]{1,0:T(8,128)S(1)}, u32[]{:S(2)}) copy-start(f32[64,4096]{1,0:T(8,128)S(1)} %get-tuple-element.9.g) | copy-start | bytes 3145732
  69.3 1.0 %copy-start.1 = (f32[64,4096]{1,0:T(8,128)}, f32[64,4096]{1,0:T(8,128)S(1)}, u32[]{:S(2)}) copy-start(f32[64,4096]{1,0:T(8,128)S(1)} %get-tuple-element.10.u) | copy-start | bytes 3145732
  70.3 1.0 %copy-start.2 = (f32[64,4096]{1,0:T(8,128)}, f32[64,4096]{1,0:T(8,128)S(1)}, u32[]{:S(2)}) copy-start(f32[64,4096]{1,0:T(8,128)S(1)} %get-tuple-element.11.d) | copy-start | bytes 3145732
  71.3 0.6 copy-start.3

commit v3 on v2

--- a/solution.py
+++ b/solution.py
@@ -10,8 +10,6 @@
 F32 = jnp.float32
 D = 4096
 ROWS = 128
-KC = 512
-NC = 512
 
 
 def nt(left, right):
@@ -183,6 +181,7 @@
     for way in both:
         x_piece(1, first(way), side(way)).wait_recv()
         go(y_other(way))
+    weights_on(2)
     for m in range(2):
         d_own(m).wait_recv()
         d_forward(m).wait_recv()
@@ -191,18 +190,10 @@
             x_piece(0, p, dy).wait_recv()
 
     def contract(m, a):
-        ACC[m] = jnp.zeros((256, 256), F32)
-
-        def step(k, carry):
-            cols = pl.ds(pl.multiple_of(k * KC, KC), KC)
-            ACC[m] += nt(arrays[a][:, :, :, cols].reshape(256, KC), W[m, :, cols])
-            return carry
-
-        lax.fori_loop(0, D // KC, step, 0)
+        ACC[m] = nt(arrays[a][...].reshape(256, D), W[m])
 
     contract(0, 0)
     contract(1, 0)
-    weights_on(2)
     gate, up = ACC[0], ACC[1]
     sig = jax.nn.sigmoid(gate)
     act = gate * sig
@@ -223,18 +214,12 @@
         return remote(SEND.at[half, m], RECV.at[half, m], gsend, grecv, half * 3 + m, at(dc=1))
 
     def grads(half, m):
-        def tile(j, carry):
-            cols = pl.ds(pl.multiple_of(j * NC, NC), NC)
-            right = arrays[m // 2][:, :, :, cols].reshape(256, NC)
-            value = nn(TT[m, pl.ds(half * 128, 128)], right)
-            SEND[half, m, :, cols] = value[:64].astype(BF)
-            if half:
-                outs[m][:, cols] = value[64:]
-            else:
-                OWNZ[m, :, cols] = value[64:]
-            return carry
-
-        lax.fori_loop(0, D // NC, tile, 0)
+        value = nn(TT[m, pl.ds(half * 128, 128)], arrays[m // 2][...].reshape(256, D))
+        SEND[half, m] = value[:64].astype(BF)
+        if half:
+            outs[m][...] = value[64:]
+        else:
+            OWNZ[m] = value[64:]
         go(grad_to_sibling(half, m))
 
     def grad_over_z(m, way):
@@ -263,11 +248,11 @@
     TT[0] = gate_term.T.astype(BF)
     TT[1] = up_term.T.astype(BF)
 
-    def dx_tile(k, carry):
-        cols = pl.ds(pl.multiple_of(k * 256, 256), 256)
-        value = nn(TERMS[:, :256], W[0, :, cols]) + nn(TERMS[:, 256:], W[1, :, cols])
-        PART[k // 2, k % 2] = value.astype(BF).reshape(4, 2, 32, 256)
-        return carry
+    def dx_half(b):
+        cols = pl.ds(b * (D // 2), D // 2)
+        value = nn(TERMS[...], W[0:2, :, cols].reshape(512, D // 2)).astype(BF)
+        for k in range(8):
+            PART[b * 4 + k // 2, k % 2] = value[:, k * 256 : (k + 1) * 256].reshape(4, 2, 32, 256)
 
     def x_hi(dx):
         return ((x + dx) % 4) // 2
@@ -313,23 +298,22 @@
         )
 
     for b in range(2):
-        lax.fori_loop(b * 8, b * 8 + 8, dx_tile, 0)
+        dx_half(b)
         for way in both:
             go(s1_opposite(b, way))
         for way in both:
             go(s1_direct(b, way))
-        if b == 0:
-            grads_over_z(2)
+    grads_over_z(2)
     grads(0, 0)
-    for way in both:
-        s1_sum(0, way)
     grads(0, 1)
-    for way in both:
-        s1_sum(1, way)
-    grads_over_z(0)
-    grads_over_z(1)
     for m in (2, 0, 1):
         grads(1, m)
+    grads_over_z(0)
+    for way in both:
+        s1_sum(0, way)
+    grads_over_z(1)
+    for way in both:
+        s1_sum(1, way)
 
     def s1_total(b):
         for way in both:
@@ -466,6 +450,7 @@
         in_specs=[vmem] * 4,
         out_specs=[hbm] * 4,
         scratch_shapes=[dma((4,))],
+        compiler_params=pltpu.CompilerParams(vmem_limit_bytes=2**20),
     )(*held)
 
 

time: 75.6 us -> 62 us (0.82)
  Pallas kernels: 71.3 us -> 61.2 us
  local copies, waits for them, and re-layouts: 3.57 us -> 0 us
    pallas_call x1, Pallas kernels: 67.7 us -> 59.5 us  [body(): pl.pallas_call(kernel, name='ffn_backward', out_shape=tuple((pltpu.VMEM(s...]
    unnamed x8 -> x0, local copies, waits for them, and re-layouts: 3.57 us -> none
    pallas_call x1, Pallas kernels: 3.57 us -> 1.7 us  [body(): pl.pallas_call(write_out, name='write_out', out_shape=tuple((jax.ShapeDty...]
where the time goes in v3:
time: 62 us; the launch traced here: 61.9 us
  Pallas kernels  61.2 us (99%)
  between operations  0.64 us (1%)
    pallas_call x1, Pallas kernels, body(): pl.pallas_call(kernel, name='ffn_backward', out_shape=tuple((pltpu.VMEM(s...  59.5 us
    pallas_call x1, Pallas kernels, body(): pl.pallas_call(write_out, name='write_out', out_shape=tuple((jax.ShapeDty...  1.7 us

profile of v3, /device:TPU:1, one launch (start us, length us, event | category | flops | bytes accessed | tf_op | source)
XLA Modules:
  0.0 61.9 jit_solution(2535161728303735454)
XLA Ops:
  0.6 59.5 %ffn_backward.1 = (bf16[128,128]{1,0:T(8,128)(2,1)S(1)}, f32[64,4096]{1,0:T(8,128)S(1)}, f32[64,4096]{1,0:T(8,128)S(1)}, f32[64,4096]{1,0:T(8,128)S(1)}) custom-call(s32[1,4]{1,0:T(1,128)} %lens.1, s32[1,4]{1,0:T(1,128)} %labs.1, bf16[128,4096]{1,0:T(8,128)(2,1)} %tok.1, bf16[128,4096]{1,0:T(8,128)(2,1)} %cot.1, bf16[64,4096]{1,0:T(8,128)(2,1)} %wg.1, ...), custom_call_target="tpu_custom_call" | custom-call | flops 4300000256 | bytes 8000000 | tf_op jit(solution)/shard_map/ffn_backward/pallas_call | solution.py:406
  60.2 1.7 %write_out.1 = (bf16[128,128]{1,0:T(8,128)(2,1)}, f32[64,4096]{1,0:T(8,128)}, f32[64,4096]{1,0:T(8,128)}, f32[64,4096]{1,0:T(8,128)}) custom-call(bf16[128,128]{1,0:T(8,128)(2,1)S(1)} %get-tuple-element.8.dx, f32[64,4096]{1,0:T(8,128)S(1)} %get-tuple-element.9.g, f32[64,4096]{1,0:T(8,128)S(1)} %get-tuple-element.10.u, f32[64,4096]{1,0:T(8,128)S(1)} %get-tuple-element.11.d), custom_call_target="tpu_custom_call" | custom-call | tf_op jit(solution)/shard_map/write_out/pallas_call | solution.py:446

commit v4 on v3

v4 whole, which is shorter than its diff:
```python
import jax
import jax.numpy as jnp
from jax import lax
from jax.experimental import pallas as pl
from jax.experimental.pallas import tpu as pltpu
from jax.sharding import PartitionSpec as P

MESH = pl.DeviceIdType.MESH
BF = jnp.bfloat16
F32 = jnp.float32
D = 4096
HALF = D // 2
ROWS = 128


def nt(left, right):
    return lax.dot_general(left, right, (((1,), (1,)), ((), ())), preferred_element_type=F32)


def nn(left, right):
    return jnp.dot(left, right, preferred_element_type=F32)


def kernel(
    lens, labs, tok, cot, wg, wu, wd,
    o_dx, o_g, o_u, o_d,
    X, C, CT, W, ACC, TERMS, TT, SEND, OWNZ, RECV, ZSEND, ZRECV,
    PART, TA, TB, RA, RB, QA, QB, R2A, R2B, F, R3,
    in_sem, ysend, yrecv, xsend, xrecv, zsend, zrecv, dsend, drecv,
    gsend, grecv, zgsend, zgrecv, s1send, s1recv, s2send, s2recv, s3send, s3recv, there,
):
    dp = lax.axis_index("dp")
    wt = lax.axis_index("weight")
    z, xh, c = dp // 4, (dp // 2) % 2, dp % 2
    y, xl = wt // 2, wt % 2
    x = xh * 2 + xl

    def at(dx=0, dy=0, dz=0, dc=0):
        xx = (x + dx) % 4
        yy = (y + dy) % 4
        zz = (z + dz) % 8
        cc = (c + dc) % 2
        return (zz * 4 + (xx // 2) * 2 + cc, yy * 2 + xx % 2)

    def remote(src, dst, ssem, rsem, k, where):
        return pltpu.make_async_remote_copy(
            src_ref=src, dst_ref=dst, send_sem=ssem.at[k], recv_sem=rsem.at[k],
            device_id=where, device_id_type=MESH,
        )

    sends = []

    def go(copy):
        copy.start()
        sends.append(copy)
        return copy

    barrier = pltpu.get_barrier_semaphore()
    column = [at(dc=1), at(dz=1), at(dz=-1)]
    partners = column + [at(dy=1), at(dy=-1), at(dx=1), at(dx=-1)]
    for who in partners:
        pl.semaphore_signal(barrier, inc=1, device_id=who, device_id_type=MESH)

    def tell(r):
        for who in column:
            pl.semaphore_signal(there.at[r], inc=1, device_id=who, device_id_type=MESH)

    def told(r):
        pl.semaphore_wait(there.at[r], len(column))

    row0 = pl.multiple_of((z % 2) * 64 + c * 32, 32)
    loads = [pltpu.make_async_copy(cot.at[pl.ds(row0, 32)], CT, in_sem.at[0])]
    for p in range(2):
        loads.append(pltpu.make_async_copy(tok.at[pl.ds(row0 + 16 * p, 16)], X.at[0, p], in_sem.at[1 + p]))
    for m, ref in enumerate((wg, wu, wd)):
        loads.append(pltpu.make_async_copy(ref, W.at[m, pl.ds(192, 64)], in_sem.at[3 + m]))
    for copy in loads:
        copy.start()

    for copy in loads[1:]:
        copy.wait()
    pl.semaphore_wait(barrier, len(partners))

    def first(way):
        return 0 if way == 1 else 1

    def side(way):
        return 3 if way == 1 else 1

    def part(a, slot, p):
        return C.at[slot, p, :, pl.ds((a - 1) * HALF, HALF)] if a else X.at[slot, p]

    def y_piece(a, p, way):
        k = first(way) * 11 + a * 2 + p
        return remote(part(a, 0, p), part(a, side(way) * 2, p), ysend, yrecv, k, at(dy=way))

    def y_next(a, way):
        p = first(way)
        k = first(way) * 11 + 6 + a
        return remote(part(a, side(way) * 2, p), part(a, 4, p), ysend, yrecv, k, at(dy=way))

    def y_other(a, way):
        p = first(way)
        k = first(way) * 11 + 8 + a
        return remote(part(a, side(way) * 2 + 1, p), part(a, 5, p), ysend, yrecv, k, at(dy=way))

    def x_piece(a, p, dy):
        k = p * 12 + dy * 3 + a
        return remote(
            part(a, dy * 2, p), part(a, dy * 2 + 1, p), xsend, xrecv, k, at(dx=1 if p == 0 else -1)
        )

    def z_weights(m, way):
        rows = (192, 64) if way == 1 else (224, 96)
        return remote(
            W.at[m, pl.ds(rows[0], 32)], W.at[m, pl.ds(rows[1], 32)],
            zsend, zrecv, m * 2 + first(way), at(dz=way),
        )

    def d_own(m):
        return remote(W.at[m, pl.ds(192, 64)], W.at[m, pl.ds(128, 64)], dsend, drecv, m, at(dc=1))

    def d_forward(m):
        return remote(W.at[m, pl.ds(64, 64)], W.at[m, pl.ds(0, 64)], dsend, drecv, 3 + m, at(dc=1))

    both = (1, -1)

    def weights_on(m):
        for way in both:
            z_weights(m, way).wait_recv()
        go(d_forward(m))

    for way in both:
        go(y_piece(0, first(way), way))
    for p in range(2):
        go(x_piece(0, p, 0))
    for m in range(3):
        for way in both:
            go(z_weights(m, way))
        if m == 0:
            for way in both:
                go(y_piece(0, 1 - first(way), way))
    for m in range(3):
        go(d_own(m))
    tell(0)

    position = lax.broadcasted_iota(jnp.int32, (32, 128), 0) + row0
    segment = jnp.zeros((32, 128), jnp.int32)
    end = lens[0, 0]
    segment = segment + (position >= end).astype(jnp.int32)
    for k in range(1, 4):
        end = end + lens[0, k]
        segment = segment + (position >= end).astype(jnp.int32)
    length = jnp.zeros((32, 128), jnp.int32)
    label = jnp.zeros((32, 128), jnp.int32)
    for k in range(4):
        length = jnp.where(segment == k, lens[0, k], length)
        label = jnp.where(segment == k, labs[0, k], label)
    factor = (1.0 + 2.0 * label.astype(F32)) * lax.rsqrt(length.astype(F32) * 4 / ROWS)
    loads[0].wait()
    for j in range(D // 128):
        cols = slice(j * 128, (j + 1) * 128)
        value = (CT[:, cols].astype(F32) * factor).astype(BF)
        C[0, 0, :, cols] = value[:16]
        C[0, 1, :, cols] = value[16:]
    for a in (1, 2):
        for p in range(2):
            go(x_piece(a, p, 0))
        for way in both:
            go(y_piece(a, first(way), way))
    for way in both:
        y_piece(0, first(way), way).wait_recv()
        go(y_next(0, way))
        go(x_piece(0, first(way), side(way)))
    for a in (1, 2):
        for way in both:
            go(y_piece(a, 1 - first(way), way))
    for way in both:
        y_piece(0, 1 - first(way), way).wait_recv()
        go(x_piece(0, 1 - first(way), side(way)))
    weights_on(0)
    told(0)
    tell(1)
    for a in (1, 2):
        for way in both:
            y_piece(a, first(way), way).wait_recv()
            go(x_piece(a, first(way), side(way)))
            go(y_next(a, way))
    for way in both:
        y_next(0, way).wait_recv()
        go(x_piece(0, first(way), 2))
    weights_on(1)
    told(1)
    tell(2)
    for a in (1, 2):
        for way in both:
            y_piece(a, 1 - first(way), way).wait_recv()
            go(x_piece(a, 1 - first(way), side(way)))
        for way in both:
            x_piece(a, first(way), side(way)).wait_recv()
            go(y_other(a, way))
    weights_on(2)
    told(2)
    tell(3)

    def contract(m, ref):
        ACC[m] = nt(ref[...].reshape(256, D), W[m])

    for m in range(2):
        d_own(m).wait_recv()
        d_forward(m).wait_recv()
    for dy in (0, 3, 1, 2):
        for p in range(2):
            x_piece(0, p, dy).wait_recv()
    contract(0, X)
    contract(1, X)
    gate, up = ACC[0], ACC[1]
    sig = jax.nn.sigmoid(gate)
    act = gate * sig
    TT[2] = (act * up).T.astype(BF)

    def weighted_here(a):
        for way in both:
            y_next(a, way).wait_recv()
        for way in both:
            x_piece(a, 1 - first(way), side(way)).wait_recv()
        for p in range(2):
            x_piece(a, p, 0).wait_recv()
        for way in both:
            y_other(a, way).wait_recv()

    outs = (o_g, o_u, o_d)

    def block_of(ref, h):
        return ref if h is None else ref.at[:, pl.ds(h * HALF, HALF)]

    def grad_to_sibling(half, m, h=None):
        k = half * 3 + m if h != 1 else 6
        return remote(
            block_of(SEND.at[half, m], h), block_of(RECV.at[half, m], h), gsend, grecv, k, at(dc=1)
        )

    def grads(half, m, h=None):
        if m == 2:
            right = C[...] if h is None else C[:, :, :, h * HALF : (h + 1) * HALF]
        else:
            right = X[...]
        value = nn(TT[m, pl.ds(half * 128, 128)], right.reshape(256, right.shape[-1]))
        block_of(SEND.at[half, m], h)[...] = value[:64].astype(BF)
        block_of(outs[m] if half else OWNZ.at[m], h)[...] = value[64:]
        go(grad_to_sibling(half, m, h))

    def grad_over_z(m, way, h=None):
        rows = pl.ds(0 if way == -1 else 32, 32)
        k = (m if h != 1 else 3) * 2 + first(way)
        return remote(
            block_of(ZSEND.at[m, rows], h), block_of(ZRECV.at[m, rows], h), zgsend, zgrecv, k, at(dz=way)
        )

    def grads_over_z(m, h=None):
        grad_to_sibling(0, m, h).wait_recv()
        mine, came = block_of(OWNZ.at[m], h), block_of(RECV.at[0, m], h)
        block_of(ZSEND.at[m], h)[...] = (mine[...] + came[...].astype(F32)).astype(BF)
        for way in both:
            go(grad_over_z(m, way, h))

    weighted_here(1)
    grads(0, 2, 0)
    weighted_here(2)
    d_own(2).wait_recv()
    d_forward(2).wait_recv()
    contract(2, C)
    grads(0, 2, 1)
    grads_over_z(2, 0)
    hidden_grad = ACC[2]
    gate, up = ACC[0], ACC[1]
    sig = jax.nn.sigmoid(gate)
    act = gate * sig
    gate_term = hidden_grad * up * sig * (1.0 + gate * (1.0 - sig))
    up_term = hidden_grad * act
    TERMS[:, :256] = gate_term.astype(BF)
    TERMS[:, 256:] = up_term.astype(BF)
    TT[0] = gate_term.T.astype(BF)
    TT[1] = up_term.T.astype(BF)

    def dx_half(b):
        cols = pl.ds(b * (D // 2), D // 2)
        value = nn(TERMS[...], W[0:2, :, cols].reshape(512, D // 2)).astype(BF)
        for k in range(8):
            PART[b * 4 + k // 2, k % 2] = value[:, k * 256 : (k + 1) * 256].reshape(4, 2, 32, 256)

    def x_hi(dx):
        return ((x + dx) % 4) // 2

    def jz(j):
        return (z + j) % 2

    def chunk(b, h, to, j):
        if b:
            return PART.at[4 + h * 2 + jz(j), x_hi(to), :, to % 2]
        return PART.at[h * 2 + jz(j), :, to]

    def along(b, way):
        return at(dx=way) if b else at(dy=way)

    def s1_opposite(b, way, j):
        h = first(way)
        return remote(chunk(b, h, 2, j), (TB if b else TA).at[j, h], s1send, s1recv, b * 12 + j * 6 + h, along(b, way))

    def s1_direct(b, way, j):
        i = first(way)
        return remote(
            chunk(b, 1 - i, way % 4, j), (RB if b else RA).at[j, i],
            s1send, s1recv, b * 12 + j * 6 + 2 + i, along(b, way),
        )

    def s1_summed(b, way, j):
        i = first(way)
        return remote(
            chunk(b, i, way % 4, j), (RB if b else RA).at[j, 2 + i],
            s1send, s1recv, b * 12 + j * 6 + 4 + i, along(b, way),
        )

    def s1_sum(b, j):
        for way in both:
            h = first(way)
            s1_opposite(b, way, j).wait_recv()
            mine = chunk(b, h, way % 4, j)
            mine[...] = (mine[...].astype(F32) + (TB if b else TA)[j, h].astype(F32)).astype(BF)
            go(s1_summed(b, way, j))
        if j == 0:
            for way in both:
                go(s1_direct(b, way, 1))

    def s1_total(b, j):
        for way in both:
            s1_direct(b, way, j).wait_recv()
        for way in both:
            s1_summed(b, way, j).wait_recv()
        came = RB if b else RA
        for h in range(2):
            total = chunk(b, h, 0, j)[...].astype(F32) + came[j, 1 - h].astype(F32) + came[j, 2 + h].astype(F32)
            (QB if b else QA)[j, h] = total.astype(BF)
        for d in (2, 1, 3):
            go(s2(b, d, j))

    def s2(b, d, j):
        if b:
            src, dst, where = QB.at[j, :, d], R2B.at[d - 1, j], at(dy=d)
        else:
            src, dst, where = QA.at[j, :, x_hi(d), d % 2], R2A.at[d - 1, j], at(dx=d)
        return remote(src, dst, s2send, s2recv, b * 6 + j * 3 + d - 1, where)

    def s2_total(b, j):
        for d in (1, 3, 2):
            s2(b, d, j).wait_recv()
        if b:
            total, came = QB[j, :, 0].astype(F32), R2B
        else:
            total, came = QA[j, :, xh, 0].astype(F32), R2A
        for i in range(3):
            total = total + came[i, j].astype(F32)
        for h in range(2):
            for k in range(2):
                F[b * 4 + h * 2 + jz(j), k] = total[h, :, k * 128 : (k + 1) * 128].astype(BF)

    def s3(dz, dc):
        k = dz * 2 + dc
        return remote(
            F.at[(z + dz) % 8, (c + dc) % 2], R3.at[k], s3send, s3recv, k, at(dz=dz, dc=dc)
        )

    for b in range(2):
        dx_half(b)
        for j in range(2):
            for way in both:
                go(s1_opposite(b, way, j))
        for way in both:
            go(s1_direct(b, way, 0))
    grads_over_z(2, 1)
    grads(0, 0)
    grads(0, 1)
    grads(1, 2)
    s1_sum(0, 0)
    s1_sum(1, 0)
    grads_over_z(0)
    grads(1, 0)
    s1_sum(0, 1)
    s1_sum(1, 1)
    grads_over_z(1)
    grads(1, 1)
    for j in range(2):
        for b in range(2):
            s1_total(b, j)

    for m in (2, 0, 1):
        grad_to_sibling(1, m).wait_recv()
        outs[m][...] += RECV[1, m].astype(F32)

    told(3)
    before = len(sends)
    for j in range(2):
        for b in range(2):
            s2_total(b, j)
        for dz in (4, 3, 5, 2, 6, 1, 7, 0):
            for dc in range(2):
                if dz % 2 == j and (dz or dc):
                    go(s3(dz, dc))
    for copy in sends[:before]:
        copy.wait_send()

    def finish(m):
        for way in both:
            for h in (0, 1) if m == 2 else (None,):
                grad_over_z(m, way, h).wait_recv()
        outs[m][...] = (outs[m][...] + ZRECV[m].astype(F32)) * (1.0 / 32.0)

    finish(2)
    finish(0)
    finish(1)
    for dz in range(8):
        for dc in range(2):
            if dz or dc:
                s3(dz, dc).wait_recv()
    for odd in range(2):
        for dc in range(2):
            total = None
            for dz in range(odd, 8, 2):
                if dz == 0 and dc == 0:
                    term = F[z, c].astype(F32)
                else:
                    term = R3[dz * 2 + dc].astype(F32)
                total = term if total is None else total + term
            row = pl.multiple_of(((z + odd) % 2) * 64 + ((c + dc) % 2) * 32, 32)
            o_dx[pl.ds(row, 32), :] = total.astype(BF)
    for copy in sends[before:]:
        copy.wait_send()


def write_out(dx, g, u, d, o_dx, o_g, o_u, o_d, sem):
    copies = [
        pltpu.make_async_copy(src, dst, sem.at[k])
        for k, (src, dst) in enumerate(((g, o_g), (u, o_u), (d, o_d), (dx, o_dx)))
    ]
    for copy in copies:
        copy.start()
    for copy in copies:
        copy.wait()


def body(tokens, cotangent, step_lengths, step_labels, gate_weight, up_weight, down_weight):
    dma = pltpu.SemaphoreType.DMA
    hbm = pl.BlockSpec(memory_space=pltpu.HBM)
    smem = pl.BlockSpec(memory_space=pltpu.SMEM)
    vmem = pl.BlockSpec(memory_space=pltpu.VMEM)
    shapes = [((128, 128), BF)] + [((64, D), F32)] * 3
    held = pl.pallas_call(
        kernel,
        name="ffn_backward",
        out_shape=tuple(pltpu.VMEM(shape, dtype) for shape, dtype in shapes),
        in_specs=[smem, smem] + [hbm] * 5,
        out_specs=[vmem] * 4,
        scratch_shapes=[
            pltpu.VMEM((8, 2, 16, D), BF),
            pltpu.VMEM((8, 2, 16, D), BF),
            pltpu.VMEM((32, D), BF),
            pltpu.VMEM((3, 256, D), BF),
            pltpu.VMEM((3, 256, 256), F32),
            pltpu.VMEM((256, 512), BF),
            pltpu.VMEM((3, 256, 256), BF),
            pltpu.VMEM((2, 3, 64, D), BF),
            pltpu.VMEM((3, 64, D), F32),
            pltpu.VMEM((2, 3, 64, D), BF),
            pltpu.VMEM((3, 64, D), BF),
            pltpu.VMEM((3, 64, D), BF),
            pltpu.VMEM((8, 2, 4, 2, 32, 256), BF),
            pltpu.VMEM((2, 2, 2, 2, 32, 256), BF),
            pltpu.VMEM((2, 2, 4, 32, 256), BF),
            pltpu.VMEM((2, 4, 2, 2, 32, 256), BF),
            pltpu.VMEM((2, 4, 4, 32, 256), BF),
            pltpu.VMEM((2, 2, 2, 2, 32, 256), BF),
            pltpu.VMEM((2, 2, 4, 32, 256), BF),
            pltpu.VMEM((3, 2, 2, 32, 256), BF),
            pltpu.VMEM((3, 2, 2, 32, 256), BF),
            pltpu.VMEM((8, 2, 32, 128), BF),
            pltpu.VMEM((16, 32, 128), BF),
            dma((6,)), dma((22,)), dma((22,)), dma((24,)), dma((24,)),
            dma((6,)), dma((6,)), dma((6,)), dma((6,)),
            dma((7,)), dma((7,)), dma((8,)), dma((8,)),
            dma((24,)), dma((24,)), dma((12,)), dma((12,)), dma((16,)), dma((16,)),
            pltpu.SemaphoreType.REGULAR((4,)),
        ],
        compiler_params=pltpu.CompilerParams(
            collective_id=0, has_side_effects=True, vmem_limit_bytes=60 * 2**20 + 2**19
        ),
        cost_estimate=pl.CostEstimate(flops=4_300_000_000, bytes_accessed=8_000_000, transcendentals=65536),
    )(step_lengths, step_labels, tokens, cotangent, gate_weight, up_weight, down_weight)
    return pl.pallas_call(
        write_out,
        name="write_out",
        out_shape=tuple(jax.ShapeDtypeStruct(shape, dtype) for shape, dtype in shapes),
        in_specs=[vmem] * 4,
        out_specs=[hbm] * 4,
        scratch_shapes=[dma((4,))],
        compiler_params=pltpu.CompilerParams(vmem_limit_bytes=2**20),
    )(*held)


def solution(mesh):
    return jax.shard_map(
        body,
        mesh=mesh,
        in_specs=(
            P("weight", None),
            P("weight", None),
            P("weight", None),
            P("weight", None),
            P(("dp", "weight"), None),
            P(("dp", "weight"), None),
            P(("dp", "weight"), None),
        ),
        out_specs=(
            P("weight", "dp"),
            P(("dp", "weight"), None),
            P(("dp", "weight"), None),
            P(("dp", "weight"), None),
        ),
        check_vma=False,
    )
```

time: 62 us -> 61.3 us (0.989)
  Pallas kernels: 61.2 us -> 60.5 us
    pallas_call x1, Pallas kernels: 59.5 us -> 58.8 us  [body(): pl.pallas_call(kernel, name='ffn_backward', out_shape=tuple((pltpu.VMEM(s...]
where the time goes in v4:
time: 61.3 us; the launch traced here: 61.2 us
  Pallas kernels  60.5 us (99%)
  between operations  0.64 us (1%)
    pallas_call x1, Pallas kernels, body(): pl.pallas_call(kernel, name='ffn_backward', out_shape=tuple((pltpu.VMEM(s...  58.8 us
    pallas_call x1, Pallas kernels, body(): pl.pallas_call(write_out, name='write_out', out_shape=tuple((jax.ShapeDty...  1.7 us

profile of v4, /device:TPU:1, one launch (start us, length us, event | category | flops | bytes accessed | tf_op | source)
XLA Modules:
  0.0 61.2 jit_solution(12021306776805479079)
XLA Ops:
  0.6 58.8 %ffn_backward.1 = (bf16[128,128]{1,0:T(8,128)(2,1)S(1)}, f32[64,4096]{1,0:T(8,128)S(1)}, f32[64,4096]{1,0:T(8,128)S(1)}, f32[64,4096]{1,0:T(8,128)S(1)}) custom-call(s32[1,4]{1,0:T(1,128)} %lens.1, s32[1,4]{1,0:T(1,128)} %labs.1, bf16[128,4096]{1,0:T(8,128)(2,1)} %tok.1, bf16[128,4096]{1,0:T(8,128)(2,1)} %cot.1, bf16[64,4096]{1,0:T(8,128)(2,1)} %wg.1, ...), custom_call_target="tpu_custom_call" | custom-call | flops 4300000256 | bytes 8000000 | tf_op jit(solution)/shard_map/ffn_backward/pallas_call | solution.py:457
  59.5 1.7 %write_out.1 = (bf16[128,128]{1,0:T(8,128)(2,1)}, f32[64,4096]{1,0:T(8,128)}, f32[64,4096]{1,0:T(8,128)}, f32[64,4096]{1,0:T(8,128)}) custom-call(bf16[128,128]{1,0:T(8,128)(2,1)S(1)} %get-tuple-element.8.dx, f32[64,4096]{1,0:T(8,128)S(1)} %get-tuple-element.9.g, f32[64,4096]{1,0:T(8,128)S(1)} %get-tuple-element.10.u, f32[64,4096]{1,0:T(8,128)S(1)} %get-tuple-element.11.d), custom_call_target="tpu_custom_call" | custom-call | tf_op jit(solution)/shard_map/write_out/pallas_call | solution.py:498

commit v5 on v4

--- a/solution.py
+++ b/solution.py
@@ -10,6 +10,7 @@
 F32 = jnp.float32
 D = 4096
 HALF = D // 2
+EARLY = 1024
 ROWS = 128
 
 
@@ -24,10 +25,10 @@
 def kernel(
     lens, labs, tok, cot, wg, wu, wd,
     o_dx, o_g, o_u, o_d,
-    X, C, CT, W, ACC, TERMS, TT, SEND, OWNZ, RECV, ZSEND, ZRECV,
+    X, C, CT, W, ACC, TERMS, TT, SEND, OWNZ, RECV, ZSEND, ZRECV, EARLYS, EARLYR,
     PART, TA, TB, RA, RB, QA, QB, R2A, R2B, F, R3,
     in_sem, ysend, yrecv, xsend, xrecv, zsend, zrecv, dsend, drecv,
-    gsend, grecv, zgsend, zgrecv, s1send, s1recv, s2send, s2recv, s3send, s3recv, there,
+    gsend, grecv, zgsend, zgrecv, s1send, s1recv, s2send, s2recv, s3send, s3recv, esend, erecv, there,
 ):
     dp = lax.axis_index("dp")
     wt = lax.axis_index("weight")
@@ -232,12 +233,21 @@
     outs = (o_g, o_u, o_d)
 
     def block_of(ref, h):
-        return ref if h is None else ref.at[:, pl.ds(h * HALF, HALF)]
+        if h is None:
+            return ref
+        return ref.at[:, EARLY:HALF] if h == 0 else ref.at[:, HALF:]
 
     def grad_to_sibling(half, m, h=None):
         k = half * 3 + m if h != 1 else 6
         return remote(
             block_of(SEND.at[half, m], h), block_of(RECV.at[half, m], h), gsend, grecv, k, at(dc=1)
+        )
+
+    def early_over_z(way, other):
+        row = 0 if way == -1 else 32
+        return remote(
+            EARLYS.at[pl.ds((64 if other == 0 else 0) + row, 32)], EARLYR.at[other, pl.ds(row, 32)],
+            esend, erecv, first(way) * 2 + other, at(dz=way, dc=other),
         )
 
     def grads(half, m, h=None):
@@ -246,6 +256,12 @@
         else:
             right = X[...]
         value = nn(TT[m, pl.ds(half * 128, 128)], right.reshape(256, right.shape[-1]))
+        if h == 0:
+            EARLYS[...] = value[:, :EARLY].astype(BF)
+            for way in both:
+                for other in (1, 0):
+                    go(early_over_z(way, other))
+            value = value[:, EARLY:]
         block_of(SEND.at[half, m], h)[...] = value[:64].astype(BF)
         block_of(outs[m] if half else OWNZ.at[m], h)[...] = value[64:]
         go(grad_to_sibling(half, m, h))
@@ -280,14 +296,14 @@
     up_term = hidden_grad * act
     TERMS[:, :256] = gate_term.astype(BF)
     TERMS[:, 256:] = up_term.astype(BF)
-    TT[0] = gate_term.T.astype(BF)
-    TT[1] = up_term.T.astype(BF)
-
-    def dx_half(b):
-        cols = pl.ds(b * (D // 2), D // 2)
-        value = nn(TERMS[...], W[0:2, :, cols].reshape(512, D // 2)).astype(BF)
-        for k in range(8):
-            PART[b * 4 + k // 2, k % 2] = value[:, k * 256 : (k + 1) * 256].reshape(4, 2, 32, 256)
+
+    def dx_part(b, j):
+        for h in range(2):
+            place = b * 4 + h * 2 + jz(j)
+            cols = pl.ds(pl.multiple_of(place * 512, 512), 512)
+            value = nn(TERMS[...], W[0:2, :, cols].reshape(512, 512)).astype(BF)
+            for k in range(2):
+                PART[place, k] = value[:, k * 256 : (k + 1) * 256].reshape(4, 2, 32, 256)
 
     def x_hi(dx):
         return ((x + dx) % 4) // 2
@@ -370,13 +386,16 @@
             F.at[(z + dz) % 8, (c + dc) % 2], R3.at[k], s3send, s3recv, k, at(dz=dz, dc=dc)
         )
 
-    for b in range(2):
-        dx_half(b)
-        for j in range(2):
+    for j in range(2):
+        for b in range(2):
+            dx_part(b, j)
             for way in both:
                 go(s1_opposite(b, way, j))
-        for way in both:
-            go(s1_direct(b, way, 0))
+            if j == 1:
+                for way in both:
+                    go(s1_direct(b, way, 0))
+    TT[0] = gate_term.T.astype(BF)
+    TT[1] = up_term.T.astype(BF)
     grads_over_z(2, 1)
     grads(0, 0)
     grads(0, 1)
@@ -413,7 +432,15 @@
         for way in both:
             for h in (0, 1) if m == 2 else (None,):
                 grad_over_z(m, way, h).wait_recv()
-        outs[m][...] = (outs[m][...] + ZRECV[m].astype(F32)) * (1.0 / 32.0)
+        done = 0
+        if m == 2:
+            for way in both:
+                for other in (1, 0):
+                    early_over_z(way, other).wait_recv()
+            come = EARLYR[0].astype(F32) + EARLYR[1].astype(F32)
+            outs[m][:, :EARLY] = (outs[m][:, :EARLY] + come) * (1.0 / 32.0)
+            done = EARLY
+        outs[m][:, done:] = (outs[m][:, done:] + ZRECV[m, :, done:].astype(F32)) * (1.0 / 32.0)
 
     finish(2)
     finish(0)
@@ -473,6 +500,8 @@
             pltpu.VMEM((2, 3, 64, D), BF),
             pltpu.VMEM((3, 64, D), BF),
             pltpu.VMEM((3, 64, D), BF),
+            pltpu.VMEM((128, EARLY), BF),
+            pltpu.VMEM((2, 64, EARLY), BF),
             pltpu.VMEM((8, 2, 4, 2, 32, 256), BF),
             pltpu.VMEM((2, 2, 2, 2, 32, 256), BF),
             pltpu.VMEM((2, 2, 4, 32, 256), BF),
@@ -488,7 +517,7 @@
             dma((6,)), dma((6,)), dma((6,)), dma((6,)),
             dma((7,)), dma((7,)), dma((8,)), dma((8,)),
             dma((24,)), dma((24,)), dma((12,)), dma((12,)), dma((16,)), dma((16,)),
-            pltpu.SemaphoreType.REGULAR((4,)),
+            dma((4,)), dma((4,)), pltpu.SemaphoreType.REGULAR((4,)),
         ],
         compiler_params=pltpu.CompilerParams(
             collective_id=0, has_side_effects=True, vmem_limit_bytes=60 * 2**20 + 2**19

time: 61.3 us -> 60.5 us (0.987)
  Pallas kernels: 60.5 us -> 59.8 us
    pallas_call x1, Pallas kernels: 58.8 us -> 58.1 us  [body(): pl.pallas_call(kernel, name='ffn_backward', out_shape=tuple((pltpu.VMEM(s...]
where the time goes in v5:
time: 60.5 us; the launch traced here: 60.4 us
  Pallas kernels  59.8 us (99%)
  between operations  0.64 us (1%)
    pallas_call x1, Pallas kernels, body(): pl.pallas_call(kernel, name='ffn_backward', out_shape=tuple((pltpu.VMEM(s...  58.1 us
    pallas_call x1, Pallas kernels, body(): pl.pallas_call(write_out, name='write_out', out_shape=tuple((jax.ShapeDty...  1.7 us

profile of v5, /device:TPU:1, one launch (start us, length us, event | category | flops | bytes accessed | tf_op | source)
XLA Modules:
  0.0 60.4 jit_solution(11213458818987514391)
XLA Ops:
  0.6 58.1 %ffn_backward.1 = (bf16[128,128]{1,0:T(8,128)(2,1)S(1)}, f32[64,4096]{1,0:T(8,128)S(1)}, f32[64,4096]{1,0:T(8,128)S(1)}, f32[64,4096]{1,0:T(8,128)S(1)}) custom-call(s32[1,4]{1,0:T(1,128)} %lens.1, s32[1,4]{1,0:T(1,128)} %labs.1, bf16[128,4096]{1,0:T(8,128)(2,1)} %tok.1, bf16[128,4096]{1,0:T(8,128)(2,1)} %cot.1, bf16[64,4096]{1,0:T(8,128)(2,1)} %wg.1, ...), custom_call_target="tpu_custom_call" | custom-call | flops 4300000256 | bytes 8000000 | tf_op jit(solution)/shard_map/ffn_backward/pallas_call | solution.py:484
  58.7 1.7 %write_out.1 = (bf16[128,128]{1,0:T(8,128)(2,1)}, f32[64,4096]{1,0:T(8,128)}, f32[64,4096]{1,0:T(8,128)}, f32[64,4096]{1,0:T(8,128)}) custom-call(bf16[128,128]{1,0:T(8,128)(2,1)S(1)} %get-tuple-element.8.dx, f32[64,4096]{1,0:T(8,128)S(1)} %get-tuple-element.9.g, f32[64,4096]{1,0:T(8,128)S(1)} %get-tuple-element.10.u, f32[64,4096]{1,0:T(8,128)S(1)} %get-tuple-element.11.d), custom_call_target="tpu_custom_call" | custom-call | tf_op jit(solution)/shard_map/write_out/pallas_call | solution.py:527

commit v6 on v5

--- a/solution.py
+++ b/solution.py
@@ -23,9 +23,9 @@
 
 
 def kernel(
-    lens, labs, tok, cot, wg, wu, wd,
+    lens_in, labs_in, tok, cot, wg, wu, wd,
     o_dx, o_g, o_u, o_d,
-    X, C, CT, W, ACC, TERMS, TT, SEND, OWNZ, RECV, ZSEND, ZRECV, EARLYS, EARLYR,
+    lens, labs, X, C, CT, W, ACC, TERMS, TT, SEND, OWNZ, RECV, ZSEND, ZRECV, EARLYS, EARLYR,
     PART, TA, TB, RA, RB, QA, QB, R2A, R2B, F, R3,
     in_sem, ysend, yrecv, xsend, xrecv, zsend, zrecv, dsend, drecv,
     gsend, grecv, zgsend, zgrecv, s1send, s1recv, s2send, s2recv, s3send, s3recv, esend, erecv, there,
@@ -75,7 +75,11 @@
         loads.append(pltpu.make_async_copy(tok.at[pl.ds(row0 + 16 * p, 16)], X.at[0, p], in_sem.at[1 + p]))
     for m, ref in enumerate((wg, wu, wd)):
         loads.append(pltpu.make_async_copy(ref, W.at[m, pl.ds(192, 64)], in_sem.at[3 + m]))
-    for copy in loads:
+    steps = [
+        pltpu.make_async_copy(lens_in, lens, in_sem.at[6]),
+        pltpu.make_async_copy(labs_in, labs, in_sem.at[7]),
+    ]
+    for copy in loads + steps:
         copy.start()
 
     for copy in loads[1:]:
@@ -145,6 +149,8 @@
         go(d_own(m))
     tell(0)
 
+    for copy in steps:
+        copy.wait()
     position = lax.broadcasted_iota(jnp.int32, (32, 128), 0) + row0
     segment = jnp.zeros((32, 128), jnp.int32)
     end = lens[0, 0]
@@ -478,16 +484,17 @@
 def body(tokens, cotangent, step_lengths, step_labels, gate_weight, up_weight, down_weight):
     dma = pltpu.SemaphoreType.DMA
     hbm = pl.BlockSpec(memory_space=pltpu.HBM)
-    smem = pl.BlockSpec(memory_space=pltpu.SMEM)
     vmem = pl.BlockSpec(memory_space=pltpu.VMEM)
     shapes = [((128, 128), BF)] + [((64, D), F32)] * 3
     held = pl.pallas_call(
         kernel,
         name="ffn_backward",
         out_shape=tuple(pltpu.VMEM(shape, dtype) for shape, dtype in shapes),
-        in_specs=[smem, smem] + [hbm] * 5,
+        in_specs=[hbm] * 7,
         out_specs=[vmem] * 4,
         scratch_shapes=[
+            pltpu.SMEM((1, 4), jnp.int32),
+            pltpu.SMEM((1, 4), jnp.int32),
             pltpu.VMEM((8, 2, 16, D), BF),
             pltpu.VMEM((8, 2, 16, D), BF),
             pltpu.VMEM((32, D), BF),
@@ -513,7 +520,7 @@
             pltpu.VMEM((3, 2, 2, 32, 256), BF),
             pltpu.VMEM((8, 2, 32, 128), BF),
             pltpu.VMEM((16, 32, 128), BF),
-            dma((6,)), dma((22,)), dma((22,)), dma((24,)), dma((24,)),
+            dma((8,)), dma((22,)), dma((22,)), dma((24,)), dma((24,)),
             dma((6,)), dma((6,)), dma((6,)), dma((6,)),
             dma((7,)), dma((7,)), dma((8,)), dma((8,)),
             dma((24,)), dma((24,)), dma((12,)), dma((12,)), dma((16,)), dma((16,)),

time: 60.5 us -> 59.9 us (0.990)
  Pallas kernels: 59.8 us -> 59.1 us
    pallas_call x1, Pallas kernels: 58.1 us -> 57.4 us  [body(): pl.pallas_call(kernel, name='ffn_backward', out_shape=tuple((pltpu.VMEM(s...]
where the time goes in v6:
time: 59.9 us; the launch traced here: 59.8 us
  Pallas kernels  59.1 us (99%)
  between operations  0.64 us (1%)
    pallas_call x1, Pallas kernels, body(): pl.pallas_call(kernel, name='ffn_backward', out_shape=tuple((pltpu.VMEM(s...  57.4 us
    pallas_call x1, Pallas kernels, body(): pl.pallas_call(write_out, name='write_out', out_shape=tuple((jax.ShapeDty...  1.7 us

profile of v6, /device:TPU:1, one launch (start us, length us, event | category | flops | bytes accessed | tf_op | source)
XLA Modules:
  0.0 59.8 jit_solution(14743328322498190284)
XLA Ops:
  0.6 57.4 %ffn_backward.1 = (bf16[128,128]{1,0:T(8,128)(2,1)S(1)}, f32[64,4096]{1,0:T(8,128)S(1)}, f32[64,4096]{1,0:T(8,128)S(1)}, f32[64,4096]{1,0:T(8,128)S(1)}) custom-call(s32[1,4]{1,0:T(1,128)} %lens_in.1, s32[1,4]{1,0:T(1,128)} %labs_in.1, bf16[128,4096]{1,0:T(8,128)(2,1)} %tok.1, bf16[128,4096]{1,0:T(8,128)(2,1)} %cot.1, bf16[64,4096]{1,0:T(8,128)(2,1)} %wg.1, ...), custom_call_target="tpu_custom_call" | custom-call | flops 4300000256 | bytes 8000000 | tf_op jit(solution)/shard_map/ffn_backward/pallas_call | solution.py:489
  58.1 1.7 %write_out.1 = (bf16[128,128]{1,0:T(8,128)(2,1)}, f32[64,4096]{1,0:T(8,128)}, f32[64,4096]{1,0:T(8,128)}, f32[64,4096]{1,0:T(8,128)}) custom-call(bf16[128,128]{1,0:T(8,128)(2,1)S(1)} %get-tuple-element.8.dx, f32[64,4096]{1,0:T(8,128)S(1)} %get-tuple-element.9.g, f32[64,4096]{1,0:T(8,128)S(1)} %get-tuple-element.10.u, f32[64,4096]{1,0:T(8,128)S(1)} %get-tuple-element.11.d), custom_call_target="tpu_custom_call" | custom-call | tf_op jit(solution)/shard_map/write_out/pallas_call | solution.py:534
